TPU v7x, 512 devices: a whole 4x8x8 slice. The times are simulated.
512 devices in a mesh: group: 2 (over core), dp: 16 (over z, y_hi), mp: 16 (over y_lo, x).
Axes of the slice: x: 4, y: 8 (y_hi: 2, y_lo: 4; y = y_hi * 4 + y_lo), z: 8, core: 2. Of those that a mesh axis runs over, the one named last changes fastest.
Arguments:
- queries: bfloat16 [1024, 4, 16384], P('dp', None, 'mp'), may hold values from -160 to 160
- cache_keys: bfloat16 [1024, 64, 1024], P(('dp', 'mp')), may hold values from -6 to 6
- cache_values: bfloat16 [1024, 64, 1024], P(('dp', 'mp')), may hold values from -6 to 6
- slot_keys: bfloat16 [1024, 4, 1024], P(('dp', 'mp')), may hold values from -6 to 6
- slot_values: bfloat16 [1024, 4, 1024], P(('dp', 'mp')), may hold values from -6 to 6
- cache_lengths: int32 [1024], P(('dp', 'mp')), may hold values from 2 to 64, as said below
- embeddings: bfloat16 [1024, 4, 16384], P('dp', None, 'mp'), may hold values from -160 to 160
- layer_low: bfloat16 [1024, 4, 16384], P('dp', None, 'mp'), may hold values from -160 to 160
- layer_mid: bfloat16 [1024, 4, 16384], P('dp', None, 'mp'), may hold values from -160 to 160
- accepted: int32 [1024], P('dp'), may hold values from 0 to 4
- join_gain: float32 [3, 16384], P(None, 'mp'), may hold values from 0.5 to 2
- norm_gain: float32 [2, 16384], P(None, 'mp'), may hold values from 0.5 to 2
- key_cotangent: bfloat16 [1024, 4, 1024], P('dp', None, 'mp'), may hold values from -64 to 64
- key_weight: float32 [1024, 2, 16384], P(('group', 'dp'), None, 'mp'), may hold values from -5 to 5
- moment_first: float32 [1024, 2, 16384], P(('group', 'dp'), None, 'mp'), may hold values from -4 to 4
- moment_second: float32 [1024, 2, 16384], P(('group', 'dp'), None, 'mp'), may hold values from 0.5 to 5
Outputs:
- key_weight_new: float32 [1024, 2, 16384], P(('group', 'dp'), None, 'mp')
- moment_first_new: float32 [1024, 2, 16384], P(('group', 'dp'), None, 'mp')
- moment_second_new: float32 [1024, 2, 16384], P(('group', 'dp'), None, 'mp')
- gain_grad: float32 [2, 16384], P(None, 'mp')
Inputs may be any that keep to these rules, and one draw needn't show every extreme that they name: `cache_lengths`: some row has exactly 64.
All inputs are finite; a program needn't handle non-finite values.
Results may differ from a plain program's by a relative error of at most 0.017.
Values may be sent and summed in bfloat16 or wider, within the bound.
A program may use at most 128 MiB of HBM per device.

v0:
```python
import jax
import jax.numpy as jnp
from jax import lax
from jax.sharding import PartitionSpec as P

HD = 128


first_beta = 0.9
second_beta = 0.95
learn_rate = 0.05
decay_rate = 0.1
adam_steps = 3
slot_decay = 0.8


def shifted(value, axis, steps):
    count = lax.axis_size(axis)
    first, last = (max(0, -steps), min(count, count - steps))
    return lax.ppermute(value, axis, [(source, source + steps) for source in range(first, last)])


def attend_rows(query_block, keys_block, values_block, new_keys, new_values, lengths):
    row_total, slot_total, full_width = query_block.shape
    cache_total = keys_block.shape[1]
    kv_width = keys_block.shape[2]
    kv_heads = kv_width // HD
    group_count = full_width // kv_width
    query_heads = query_block.reshape(row_total, slot_total, kv_heads, group_count, HD)
    key_heads = keys_block.reshape(row_total, cache_total, kv_heads, HD)
    value_heads = values_block.reshape(row_total, cache_total, kv_heads, HD)
    new_key_heads = new_keys.reshape(row_total, slot_total, kv_heads, HD)
    new_value_heads = new_values.reshape(row_total, slot_total, kv_heads, HD)
    factor = HD ** (-0.5)
    cache_scores = (
        jnp.einsum("rskgd,rpkd->rskgp", query_heads, key_heads, preferred_element_type=jnp.float32)
        * factor
    )
    slot_scores = (
        jnp.einsum(
            "rskgd,rukd->rskgu", query_heads, new_key_heads, preferred_element_type=jnp.float32
        )
        * factor
    )
    cache_live = (jnp.arange(cache_total)[None, :] < lengths[:, None])[:, None, None, None, :]
    slot_live = (jnp.arange(slot_total)[None, :] <= jnp.arange(slot_total)[:, None])[
        None, :, None, None, :
    ]
    lowest = jnp.float32(-1e30)
    highest = jnp.maximum(
        jnp.max(jnp.where(cache_live, cache_scores, lowest), axis=-1),
        jnp.max(jnp.where(slot_live, slot_scores, lowest), axis=-1),
    )[..., None]
    cache_exps = jnp.where(cache_live, jnp.exp(cache_scores - highest), 0.0)
    slot_exps = jnp.where(slot_live, jnp.exp(slot_scores - highest), 0.0)
    totals = jnp.sum(cache_exps, axis=-1, keepdims=True) + jnp.sum(
        slot_exps, axis=-1, keepdims=True
    )
    cache_probs = (cache_exps / totals).astype(jnp.bfloat16)
    slot_probs = (slot_exps / totals).astype(jnp.bfloat16)
    mixed = jnp.einsum(
        "rskgp,rpkd->rskgd", cache_probs, value_heads, preferred_element_type=jnp.float32
    )
    mixed = mixed + jnp.einsum(
        "rskgu,rukd->rskgd", slot_probs, new_value_heads, preferred_element_type=jnp.float32
    )
    return mixed.reshape(row_total, slot_total, full_width).astype(jnp.bfloat16)


def shards(
    queries,
    cache_keys,
    cache_values,
    slot_keys,
    slot_values,
    cache_lengths,
    embeddings,
    layer_low,
    layer_mid,
    accepted,
    join_gain,
    norm_gain,
    key_cotangent,
    key_weight,
    moment_first,
    moment_second,
):
    serving = lax.axis_index("group") == 0
    trainer = jnp.logical_not(serving)
    rows_here, slot_total, width_here = embeddings.shape
    token_total = rows_here * slot_total
    full_width = width_here * lax.axis_size("mp")
    local_queries = lax.all_to_all(queries, "mp", split_axis=0, concat_axis=2, tiled=True)
    attended = lax.cond(
        serving,
        lambda: attend_rows(
            local_queries, cache_keys, cache_values, slot_keys, slot_values, cache_lengths
        ),
        lambda: jnp.zeros(local_queries.shape, jnp.bfloat16),
    )
    spread = lax.all_to_all(attended, "mp", split_axis=2, concat_axis=0, tiled=True)
    top_layer = shifted(spread, "group", 1)
    embed_float = embeddings.astype(jnp.float32)
    low_float = layer_low.astype(jnp.float32)
    mid_float = layer_mid.astype(jnp.float32)
    top_float = top_layer.astype(jnp.float32)
    embed_sq, low_sq, mid_sq, top_sq = lax.psum(
        (
            jnp.sum(embed_float * embed_float, axis=-1),
            jnp.sum(low_float * low_float, axis=-1),
            jnp.sum(mid_float * mid_float, axis=-1),
            jnp.sum(top_float * top_float, axis=-1),
        ),
        "mp",
    )
    normal_embed = embed_float * lax.rsqrt(embed_sq / full_width + 1e-05)[..., None]
    normal_low = low_float * lax.rsqrt(low_sq / full_width + 1e-05)[..., None]
    normal_mid = mid_float * lax.rsqrt(mid_sq / full_width + 1e-05)[..., None]
    normal_top = top_float * lax.rsqrt(top_sq / full_width + 1e-05)[..., None]
    joined = join_gain[0] * normal_low + join_gain[1] * normal_mid + join_gain[2] * normal_top
    joined_sq = lax.psum(jnp.sum(joined * joined, axis=-1), "mp")
    normal_joined = joined * lax.rsqrt(joined_sq / full_width + 1e-05)[..., None]
    draft_input = jnp.stack([norm_gain[0] * normal_embed, norm_gain[1] * normal_joined], axis=2)
    draft_input = draft_input.astype(jnp.bfloat16).reshape(token_total, 2 * width_here)
    cotangent = lax.all_gather(key_cotangent, "mp", axis=2, tiled=True)
    slot_index = jnp.arange(slot_total, dtype=jnp.int32)
    slot_weight = jnp.where(
        slot_index[None, :] < accepted[:, None],
        jnp.float32(slot_decay) ** slot_index.astype(jnp.float32)[None, :],
        0.0,
    )
    key_total = cotangent.shape[2]
    scaled = (
        (slot_weight[:, :, None] * cotangent.astype(jnp.float32))
        .astype(jnp.bfloat16)
        .reshape(token_total, key_total)
    )
    grad_scale = (2.0 * full_width) ** (-0.5)
    shard_cols = key_weight.shape[0]
    row_count = lax.axis_size(("group", "dp")) * shard_cols

    def compute_term():
        return (
            lax.dot_general(
                scaled, draft_input, (((0,), (0,)), ((), ())), preferred_element_type=jnp.float32
            )
            * grad_scale
        )

    grad_flat = lax.psum_scatter(
        lax.cond(
            trainer, compute_term, lambda: jnp.zeros((row_count, draft_input.shape[1]), jnp.float32)
        ).astype(jnp.bfloat16),
        ("group", "dp"),
        scatter_dimension=0,
        tiled=True,
    ).astype(jnp.float32)
    gradient = grad_flat.reshape(key_weight.shape)
    weight_copy = key_weight.astype(jnp.bfloat16)
    normals = jnp.stack([normal_embed, normal_joined], axis=2).reshape(token_total, 2, width_here)
    running = jnp.zeros((token_total, 2 * width_here), jnp.float32)
    shard_piece = lax.all_gather(weight_copy, ("group", "dp"), axis=0, tiled=True)

    def compute_piece():
        flat_piece = shard_piece.reshape(shard_piece.shape[0], 2 * width_here)
        return jnp.dot(scaled, flat_piece, preferred_element_type=jnp.float32) * grad_scale

    input_grad = lax.cond(trainer, compute_piece, lambda: running)
    local_gain = jnp.sum(input_grad.reshape(token_total, 2, width_here) * normals, axis=0)
    local_gain = jnp.where(trainer, local_gain, 0.0)
    gain_grad = lax.psum(local_gain, ("group", "dp"))
    moment_first_new = first_beta * moment_first + (1.0 - first_beta) * gradient
    moment_second_new = second_beta * moment_second + (1.0 - second_beta) * gradient * gradient
    corrected_first = moment_first_new / (1.0 - first_beta**adam_steps)
    corrected_second = moment_second_new / (1.0 - second_beta**adam_steps)
    direction = corrected_first / (jnp.sqrt(corrected_second) + 1e-08)
    key_weight_new = key_weight - learn_rate * (direction + decay_rate * key_weight)
    return (key_weight_new, moment_first_new, moment_second_new, gain_grad)


def solution(mesh):
    return jax.shard_map(
        shards,
        mesh=mesh,
        in_specs=(
            P("dp", None, "mp"),
            P(("dp", "mp"), None, None),
            P(("dp", "mp"), None, None),
            P(("dp", "mp"), None, None),
            P(("dp", "mp"), None, None),
            P(("dp", "mp")),
            P("dp", None, "mp"),
            P("dp", None, "mp"),
            P("dp", None, "mp"),
            P("dp"),
            P(None, "mp"),
            P(None, "mp"),
            P("dp", None, "mp"),
            P(("group", "dp"), None, "mp"),
            P(("group", "dp"), None, "mp"),
            P(("group", "dp"), None, "mp"),
        ),
        out_specs=(
            P(("group", "dp"), None, "mp"),
            P(("group", "dp"), None, "mp"),
            P(("group", "dp"), None, "mp"),
            P(None, "mp"),
        ),
        check_vma=False,
    )
```

profile of v0, /device:TPU:1, one launch (start us, length us, event | category | flops | bytes accessed | tf_op | source)
XLA Modules:
  0.0 654.8 jit_solution(17925819034823134941)
XLA Ops:
  7.2 8.0 %all-to-all-start = ((bf16[64,4,1024]{2,1,0:T(4,128)(2,1)}), bf16[64,4,1024]{2,1,0:T(4,128)(2,1)S(1)}, u32[]{:S(2)}, u32[]{:S(2)}) async-start(bf16[64,4,1024]{2,1,0:T(4,128)(2,1)} %param.22), calls=%async_computation | async-start | bytes 1048576 | tf_op jit(solution)/shard_map/all_to_all | solution.py:93
  15.2 1.0 copy.112
  16.2 11.5 %all-to-all-done = bf16[64,4,1024]{2,1,0:T(4,128)(2,1)S(1)} async-done(((bf16[64,4,1024]{2,1,0:T(4,128)(2,1)}), bf16[64,4,1024]{2,1,0:T(4,128)(2,1)S(1)}, u32[]{:S(2)}, u32[]{:S(2)}) %all-to-all-start) | async-done | bytes 524320 | tf_op jit(solution)/shard_map/all_to_all | solution.py:93
  27.6 0.1 conditional.3
  27.6 0.1 broadcast.86
  27.8 16.2 %copy.106 = bf16[4,4,16384]{1,0,2:T(4,128)(2,1)} copy(bf16[4,4,16384]{2,1,0:T(4,128)(2,1)S(1)} %get-tuple-element.108) | data formatting | bytes 1048576 | tf_op jit(solution)/shard_map/cond | solution.py:94
  44.0 31.8 %reshape.152 = bf16[16,2,8192]{2,1,0:T(2,128)(2,1)} reshape(bf16[16384,4,4]{2,1,0:T(4,128)(2,1)} %bitcast.67) | data formatting | bytes 1048576
  75.8 6.2 all-to-all-start.1
  82.1 42.2 %all_gather.6 = bf16[64,4,1024]{0,1,2:T(4,128)(2,1)S(1)} all-gather(bf16[64,4,64]{0,1,2:T(4,128)(2,1)S(1)} %copy.112), channel_id=1, replica_groups=mesh['group'=2,'dp'=16,'mp'=16] {'mp'}, dimensions={2}, use_global_device_ids=true | all-gather | bytes 557056 | tf_op jit(solution)/shard_map/all_gather | solution.py:125
  124.3 0.6 copy.113
  125.0 0.3 fusion.23
  125.3 0.3 fusion.27
  125.7 0.9 multiply_convert_fusion
  126.7 37.1 %reshape.153 = bf16[16384,4,4]{2,1,0:T(4,128)(2,1)} reshape(bf16[16,2,8192]{2,1,0:T(2,128)(2,1)S(1)} %all-to-all-done.1) | data formatting | bytes 1048576
  163.8 24.7 %copy.107 = bf16[16,4,4,1024]{3,2,1,0:T(4,128)(2,1)} copy(bf16[16,4,4,1024]{2,1,3,0:T(4,128)(2,1)} %bitcast.68) | data formatting | bytes 1048576 | tf_op jit(solution)/shard_map/all_to_all | solution.py:101
  188.5 1.4 collective-permute-start
  189.9 0.3 fusion.22
  190.5 0.4 copy.114
  190.9 0.9 reshape.143
  191.9 14.7 %collective-permute-done = bf16[64,4,1024]{2,1,0:T(4,128)(2,1)S(1)} collective-permute-done((bf16[64,4,1024]{2,1,0:T(4,128)(2,1)}, bf16[64,4,1024]{2,1,0:T(4,128)(2,1)S(1)}, u32[]{:S(2)}, u32[]{:S(2)}) %collective-permute-start) | collective-permute-done | bytes 524320 | tf_op jit(solution)/shard_map/ppermute | solution.py:20
  206.6 0.3 fusion.29
  207.0 32.5 %all-reduce.1 = (f32[64,4]{0,1:T(4,128)S(1)}, f32[64,4]{0,1:T(4,128)S(1)}, f32[64,4]{0,1:T(4,128)S(1)}) all-reduce(f32[64,4]{0,1:T(4,128)S(1)} %copy.108, f32[64,4]{0,1:T(4,128)S(1)} %copy.103, f32[64,4]{0,1:T(4,128)S(1)} %copy.101), channel_id=1, replica_groups=mesh['group'=2,'dp'=16,'mp'=16] {'mp'}, use_global_device_ids=true, to_apply=%region_13.14 | all-reduce | flops 768 | bytes 6144 | tf_op jit(solution)/shard_map/psum | solution.py:107
  239.7 0.1 copy.102
  239.8 1.2 multiply_reduce_fusion.1
  241.1 31.7 %all-reduce = (f32[64,4]{0,1:T(4,128)S(1)}, f32[64,4]{0,1:T(4,128)S(1)}) all-reduce(f32[64,4]{0,1:T(4,128)S(1)} %copy.110, f32[64,4]{0,1:T(4,128)S(1)} %copy.99), channel_id=1, replica_groups=mesh['group'=2,'dp'=16,'mp'=16] {'mp'}, use_global_device_ids=true, to_apply=%region_15.16 | all-reduce | flops 512 | bytes 4096 | tf_op jit(solution)/shard_map/psum | solution.py:121
  273.0 1.1 broadcast_multiply_fusion.1
  274.1 1.1 stack.21
  275.2 0.3 broadcast_multiply_fusion.2
  275.5 1.1 stack.20
  276.6 2.4 pad_maximum_fusion
  279.1 3.5 conditional.4
  279.1 0.3 copy.127
  279.4 3.2 convolution_multiply_fusion.2
  282.6 0.3 all-gather.2.cloned.1.call-start
  282.9 158.4 %reduce-scatter.2.cloned.1.call-done = bf16[32,2048]{1,0:T(8,128)(2,1)} async-done(((bf16[1024,2048]{1,0:T(8,128)(2,1)}), bf16[32,2048]{1,0:T(8,128)(2,1)}) %reduce-scatter.2.cloned.1.call-update) | async-done | bytes 131088 | tf_op jit(solution)/shard_map/reduce_scatter | solution.py:150
  441.3 1.2 reshape.147
  442.5 1.8 multiply_subtract_fusion
  444.4 2.4 stack.28
  446.8 0.2 convert_multiply_fusion.6
  447.0 2.4 stack.27
  449.4 3.1 pad_maximum_fusion.1
  452.6 0.9 copy.129
  453.5 99.8 %all-gather.2.cloned.1.call-done = bf16[1024,2,1024]{2,1,0:T(2,128)(2,1)} async-done(((bf16[32,2,1024]{2,1,0:T(2,128)(2,1)}), bf16[1024,2,1024]{2,1,0:T(2,128)(2,1)}) %all-gather.2.cloned.1.call-update) | async-done | bytes 4194320 | tf_op jit(solution)/shard_map/all_gather | solution.py:162
  553.3 6.3 conditional.5
  553.3 3.6 copy.128
  556.9 2.6 convolution_multiply_fusion.3
  559.5 1.8 multiply_reduce_fusion
  561.4 86.6 %psum.47 = f32[2,1024]{1,0:T(2,128)} all-reduce(f32[2,1024]{1,0:T(2,128)S(1)} %select_n.38), channel_id=1, replica_groups=mesh['group'=2,'dp'=16,'mp'=16] {'group','dp'}, use_global_device_ids=true, to_apply=%region_22.23 | all-reduce | flops 2048 | bytes 16384 | tf_op jit(solution)/shard_map/psum | solution.py:171
  (49 shorter events, 1.0 us)
Async XLA Ops:
  7.2 20.4 %all-to-all-start = ((bf16[64,4,1024]{2,1,0:T(4,128)(2,1)}), bf16[64,4,1024]{2,1,0:T(4,128)(2,1)S(1)}, u32[]{:S(2)}, u32[]{:S(2)}) async-start(bf16[64,4,1024]{2,1,0:T(4,128)(2,1)} %param.22), calls=%async_computation | async-start | bytes 1048576 | tf_op jit(solution)/shard_map/all_to_all | solution.py:93
  75.8 49.1 %copy-start.1 = (bf16[64,4,1024]{2,1,0:T(4,128)(2,1)S(1)}, bf16[64,4,1024]{2,1,0:T(4,128)(2,1)}, u32[]{:S(2)}) copy-start(bf16[64,4,1024]{2,1,0:T(4,128)(2,1)} %param.29) | copy-start | bytes 1572868
  75.8 49.5 %copy-start = (bf16[64,4,1024]{2,1,0:T(4,128)(2,1)S(1)}, bf16[64,4,1024]{2,1,0:T(4,128)(2,1)}, u32[]{:S(2)}) copy-start(bf16[64,4,1024]{2,1,0:T(4,128)(2,1)} %param.30) | copy-start | bytes 1572868
  75.8 50.9 %all-to-all-start.1 = ((bf16[16,2,8192]{2,1,0:T(2,128)(2,1)}), bf16[16,2,8192]{2,1,0:T(2,128)(2,1)S(1)}, u32[]{:S(2)}, u32[]{:S(2)}) async-start(bf16[16,2,8192]{2,1,0:T(2,128)(2,1)} %reshape.152), calls=%async_computation.1 | async-start | bytes 1048576 | tf_op jit(solution)/shard_map/all_to_all | solution.py:101
  82.0 43.6 %copy-start.14 = (s32[64]{0:T(128)S(1)}, s32[64]{0:T(128)}, u32[]{:S(2)}) copy-start(s32[64]{0:T(128)} %param.31) | copy-start | bytes 772
  82.0 359.3 %reduce-scatter.2.cloned.1.call-start = ((), (), s32[]{:S(2)}) async-start(), calls=%async_computation.3 | async-start | bytes 4325376 | tf_op jit(solution)/shard_map/reduce_scatter | solution.py:150
  163.8 26.1 %copy-start.2 = (bf16[64,4,1024]{2,1,0:T(4,128)(2,1)S(1)}, bf16[64,4,1024]{2,1,0:T(4,128)(2,1)}, u32[]{:S(2)}) copy-start(bf16[64,4,1024]{2,1,0:T(4,128)(2,1)} %param.28) | copy-start | bytes 1572868
  163.8 26.7 %copy-start.4 = (bf16[64,4,1024]{2,0,1:T(8,128)(2,1)S(1)}, bf16[64,4,1024]{2,0,1:T(8,128)(2,1)}, u32[]{:S(2)}) copy-start(bf16[64,4,1024]{2,0,1:T(8,128)(2,1)} %multiply_convert_fusion) | copy-start | bytes 1572868
  188.5 3.4 copy-start.13
  188.5 3.4 copy-start.12
  188.5 18.1 %collective-permute-start = (bf16[64,4,1024]{2,1,0:T(4,128)(2,1)}, bf16[64,4,1024]{2,1,0:T(4,128)(2,1)S(1)}, u32[]{:S(2)}, u32[]{:S(2)}) collective-permute-start(bf16[64,4,1024]{2,1,0:T(4,128)(2,1)} %bitcast.20), channel_id=1, source_target_pairs={{0,256},{1,257},{2,258},{3,259},{4,260},{5,261},{6,262},{7,263},{8... | collective-permute-start | bytes 1572872 | tf_op jit(solution)/shard_map/ppermute | solution.py:20
  276.6 2.5 copy-start.7
  282.6 159.9 %copy-start.9 = (f32[32,2,1024]{2,1,0:T(2,128)S(1)}, f32[32,2,1024]{2,1,0:T(2,128)}, u32[]{:S(2)}) copy-start(f32[32,2,1024]{2,1,0:T(2,128)} %param.35) | copy-start | bytes 786436
  282.6 159.9 %copy-start.10 = (f32[32,2,1024]{2,1,0:T(2,128)S(1)}, f32[32,2,1024]{2,1,0:T(2,128)}, u32[]{:S(2)}) copy-start(f32[32,2,1024]{2,1,0:T(2,128)} %param.36) | copy-start | bytes 786436
  282.6 159.9 %copy-start.11 = (f32[32,2,1024]{2,1,0:T(2,128)S(1)}, f32[32,2,1024]{2,1,0:T(2,128)}, u32[]{:S(2)}) copy-start(f32[32,2,1024]{2,1,0:T(2,128)} %param.37) | copy-start | bytes 786436
  282.6 270.6 %all-gather.2.cloned.1.call-start = ((), (), s32[]{:S(2)}) async-start(), calls=%async_computation.4 | async-start | bytes 4325376 | tf_op jit(solution)/shard_map/all_gather | solution.py:162
  446.8 2.7 copy-start.3
  452.6 100.7 %copy-start.8 = (bf16[256,1024]{1,0:T(8,128)(2,1)S(1)}, bf16[256,1024]{1,0:T(8,128)(2,1)}, u32[]{:S(2)}) copy-start(bf16[256,1024]{1,0:T(8,128)(2,1)} %reshape.143) | copy-start | bytes 1572868
Sparse Core Ops, SparseCore 0:
  282.8 158.5 reduce-scatter.1
  445.2 108.0 all-gather.1
where the time goes:
time: 656 us; the launch traced here: 655 us
  waiting for transfers between devices  284 us (43%)
  blocking collectives  193 us (29%)
  local copies, waits for them, and re-layouts  127 us (19%)
  starting transfers between devices  15.9 us (2%)
  other arithmetic  14.5 us (2%)
  between operations  14.3 us (2%)
    reduce_scatter x1, waiting for transfers between devices, shards(): lax.psum_scatter(lax.cond(trainer, compute_term, lambda: jnp.zeros((row_c...  158 us
    all_gather x1, waiting for transfers between devices, shards(): lax.all_gather(weight_copy, ('group', 'dp'), axis=0, tiled=True)  99.8 us
    psum x1, blocking collectives, shards(): gain_grad = lax.psum(local_gain, ('group', 'dp'))  86.6 us
    unnamed x30, local copies, waits for them, and re-layouts  70.8 us
    all_gather x1, blocking collectives, shards(): cotangent = lax.all_gather(key_cotangent, 'mp', axis=2, tiled=True)  42.2 us
    psum x1, blocking collectives, shards(): lax.psum((jnp.sum(embed_float * embed_float, axis=-1), jnp.sum(low_float...  32.5 us
    psum x1, blocking collectives, shards(): joined_sq = lax.psum(jnp.sum(joined * joined, axis=-1), 'mp')  31.7 us
    all_to_all x1, local copies, waits for them, and re-layouts, shards(): lax.all_to_all(attended, 'mp', split_axis=2, concat_axis=0, tiled=True)  24.7 us
  transfers between devices with their start and end apart: 5, of which 4 were waited for; matrix products, arithmetic and copies ran while one was open for 2% of the time, Pallas kernels for 0%

commit v1 on v0

v1 whole, which is shorter than its diff:
```python
import functools

import jax
import jax.numpy as jnp
from jax import lax
from jax.experimental import pallas as pl
from jax.experimental.pallas import tpu as pltpu
from jax.sharding import PartitionSpec as P

HD = 128
SUB = 8
EPS = 1e-05
first_beta = 0.9
second_beta = 0.95
learn_rate = 0.05
decay_rate = 0.1
adam_steps = 3
slot_decay = 0.8
MESH = pl.DeviceIdType.MESH
F32 = jnp.float32
BF16 = jnp.bfloat16


def native(x):
    rows, slots, width = x.shape
    x = x.reshape(rows, slots, width // HD, HD).transpose(0, 2, 1, 3)
    return x.reshape(rows * (width // HD) * slots, HD)


def from_native(y, rows, slots, width):
    y = y.reshape(rows, width // HD, slots, HD).transpose(0, 2, 1, 3)
    return y.reshape(rows, slots, width)


def dot_nt(a, b, **kw):
    return lax.dot_general(a, b, (((1,), (1,)), ((), ())), preferred_element_type=F32, **kw)


def swap_halves(x):
    return jnp.concatenate([x[:, 4:], x[:, :4]], axis=1)


def kernel(
    dims,
    q_hbm, ck_hbm, cv_hbm, sk_ref, sv_ref, len_ref, em_hbm, lo_hbm, mi_hbm, cot_hbm,
    jg_ref, ng_ref, ngn_ref, w_hbm, m1_hbm, m2_hbm,
    w_out, m1_out, m2_out, gain_out,
    rxq, kbuf, vbuf, outb, emb, lob, mib, topb, cbuf, wbuf, m1buf, m2buf,
    gpat, zbuf, ssend, srecv, red, vx, ax, tb, sring, rring, sy, ry, gs1, gr1, gs2, gr2,
    lsem, q_s, q_r, c_s, c_r, o_s, o_r, s_s, s_r, red_s, red_r, top_s, top_r,
    ring_s, ring_r, y_s, y_r, g1_s, g1_r, g2_s, g2_r,
):
    NZ, NY, MP, KVH, F, D, HC, SH = dims
    LT = F // HD
    T = MP * 4 * SUB // 2
    TH = T // 2
    H = NZ // 2
    RB = NY * SH
    g = lax.axis_index("group")
    d = lax.axis_index("dp")
    m = lax.axis_index("mp")
    z, y = d // NY, lax.rem(d, NY)

    def at(gg=None, dd=None, mm=None):
        return (g if gg is None else gg, d if dd is None else dd, m if mm is None else mm)

    def zdev(zz):
        return lax.rem(zz + NZ, NZ) * NY + y

    def remote(src, dst, s, r, dev):
        return pltpu.make_async_remote_copy(
            src_ref=src, dst_ref=dst, send_sem=s, recv_sem=r, device_id=dev, device_id_type=MESH
        )

    def rem_mp(j):
        return lax.rem(m + j, MP)

    loads = {
        "k": pltpu.make_async_copy(ck_hbm.at[pl.ds(2 * g, 2)], kbuf, lsem.at[0]),
        "v": pltpu.make_async_copy(cv_hbm.at[pl.ds(2 * g, 2)], vbuf, lsem.at[1]),
        "lo": pltpu.make_async_copy(lo_hbm, lob, lsem.at[2]),
        "mi": pltpu.make_async_copy(mi_hbm, mib, lsem.at[3]),
        "em": pltpu.make_async_copy(em_hbm, emb, lsem.at[4]),
        "w": pltpu.make_async_copy(w_hbm, wbuf, lsem.at[5]),
        "m1": pltpu.make_async_copy(m1_hbm, m1buf, lsem.at[6]),
        "m2": pltpu.make_async_copy(m2_hbm, m2buf, lsem.at[7]),
        "q": pltpu.make_async_copy(q_hbm.at[m, g], rxq.at[m], lsem.at[8]),
    }
    for key in ("lo", "mi", "em", "q", "k", "v", "w", "m1", "m2"):
        loads[key].start()

    bar = pltpu.get_barrier_semaphore()

    def greet(j, c):
        pl.semaphore_signal(bar, inc=1, device_id=at(mm=rem_mp(j)), device_id_type=MESH)
        return c

    lax.fori_loop(1, MP, greet, 0)

    def greet_z(j, c):
        pl.semaphore_signal(bar, inc=1, device_id=at(dd=zdev(z + j)), device_id_type=MESH)
        return c

    lax.fori_loop(1, NZ, greet_z, 0)
    pl.semaphore_signal(bar, inc=1, device_id=at(gg=1 - g), device_id_type=MESH)
    greeted = MP - 1 + NZ - 1 + 1
    if NY == 2:
        pl.semaphore_signal(bar, inc=1, device_id=at(dd=z * NY + 1 - y), device_id_type=MESH)
        pl.semaphore_signal(bar, inc=1, device_id=at(gg=1 - g, dd=z * NY + 1 - y), device_id_type=MESH)
        greeted += 2
    pl.semaphore_wait(bar, greeted)

    def q_copy(j):
        dst = rem_mp(j)
        return remote(q_hbm.at[dst, g], rxq.at[m], q_s.at[j], q_r.at[m], at(mm=dst))

    def q_start(j, c):
        q_copy(j).start()
        return c

    lax.fori_loop(1, MP, q_start, 0)

    half = MP // 2
    mine = lax.rem(m, half)
    sends_cot = (m // half) == g

    def c_copy(j):
        return remote(cot_hbm, cbuf.at[mine], c_s.at[j], c_r.at[mine], at(mm=rem_mp(j)))

    own_cot = pltpu.make_async_copy(cot_hbm, cbuf.at[mine], c_s.at[0])

    @pl.when(sends_cot)
    def _():
        own_cot.start()

        def c_start(j, c):
            c_copy(j).start()
            return c

        lax.fori_loop(1, MP, c_start, 0)

    sub8 = lax.broadcasted_iota(jnp.int32, (1, SUB, HD), 1) < 4
    for a in range(3):
        for lp in range(LT // 2):
            lower = jg_ref[a : a + 1, 2 * lp * HD : (2 * lp + 1) * HD]
            upper = jg_ref[a : a + 1, (2 * lp + 1) * HD : (2 * lp + 2) * HD]
            gpat[a, lp] = jnp.where(sub8[0], lower, upper)

    def native_block(ref, i):
        return ref.astype(F32).reshape(2, LT // 2, SUB, HD)

    def fold(p):
        t = jnp.sum(p, axis=1)
        t = t + swap_halves(t)
        return jnp.where(sub8[0], t[0], t[1])

    zbuf[...] = jnp.zeros_like(zbuf)
    loads["lo"].wait()
    loads["mi"].wait()
    loads["em"].wait()
    g0, g1, g2 = gpat[0], gpat[1], gpat[2]

    def stats0(i, c):
        e = native_block(emb[i, g], i)
        l = native_block(lob[i, g], i)
        v = native_block(mib[i, g], i)
        gl, gv = l * g0, v * g1
        rows = pl.ds(pl.multiple_of(i * SUB, SUB), SUB)
        for n, p in enumerate((e * e, l * l, v * v, gl * gl, gv * gv, gl * gv)):
            zbuf[n, rows, :] = fold(p)
        return c

    lax.fori_loop(0, MP, stats0, 0)

    def row_sums(count):
        total = jnp.zeros((SUB, TH), F32)
        for n in range(count):
            pick = (lax.broadcasted_iota(jnp.int32, (SUB, HD), 0) == n).astype(F32)
            total = total + dot_nt(pick, zbuf[n], precision=lax.Precision.HIGHEST)
        return total

    def s_copy(ph, j):
        return remote(ssend.at[ph], srecv.at[ph, m], s_s.at[ph, j], s_r.at[ph, m], at(mm=rem_mp(j)))

    def s_begin(ph, count):
        ssend[ph] = row_sums(count)

        def go(j, c):
            s_copy(ph, j).start()
            return c

        lax.fori_loop(1, MP, go, 0)

    def red_copy(ph):
        return remote(red.at[ph, g], red.at[ph, g], red_s.at[ph], red_r.at[ph], at(gg=1 - g))

    def s_reduce(ph):
        def add(j, total):
            src = rem_mp(j)
            remote(
                ssend.at[ph], srecv.at[ph, src], s_s.at[ph, j], s_r.at[ph, src], at(mm=src)
            ).wait_recv()
            return total + srecv[ph, src]

        red[ph, g] = lax.fori_loop(1, MP, add, ssend[ph])
        red_copy(ph).start()

    s_begin(0, 6)

    def relayout(x, col, gg, n):
        x = x.astype(F32).reshape(2, LT // 2, SUB, HD)
        a, b = x[0], x[1]
        even = jnp.where(sub8, a, swap_halves(b))
        odd = jnp.where(sub8, swap_halves(a), b)
        return even, odd

    def relayout_all(n, load, gg):
        def two(i, c):
            parts = [relayout(load(2 * i + h, gg), 0, gg, n) for h in range(2)]
            rows = pl.ds(pl.multiple_of(gg * TH + i * 2 * SUB, 2 * SUB), 2 * SUB)
            for lp in range(LT // 2):
                for k in range(2):
                    tile = jnp.concatenate([parts[0][k][lp], parts[1][k][lp]], axis=0)
                    lt = 2 * lp + k
                    vx[n, rows, lt * HD : (lt + 1) * HD] = tile.astype(BF16)
            return c

        lax.fori_loop(0, MP // 2, two, 0)

    for gg in range(2):
        relayout_all(0, lambda i, gg: emb[i, gg], gg)

    loads["k"].wait()
    loads["v"].wait()
    loads["q"].wait()

    def q_wait(j, c):
        src = rem_mp(j)
        remote(q_hbm.at[src, g], rxq.at[src], q_s.at[j], q_r.at[src], at(mm=src)).wait_recv()
        return c

    lax.fori_loop(1, MP, q_wait, 0)

    CP = 64
    SR = KVH * 4
    QR = 32
    rowi = lax.broadcasted_iota(jnp.int32, (2 * QR, HD), 0)
    coli = lax.broadcasted_iota(jnp.int32, (2 * QR, HD), 1)
    slot_of = lax.rem(rowi, 4)
    scol = coli - CP
    in_slots = (scol >= 0) & (scol < SR) & (lax.rem(scol, 4) <= slot_of)
    pad = jnp.zeros((HD - CP - SR, HD), BF16)

    def attend(r, c):
        length = len_ref[2 * g + r]
        srows = pl.ds(pl.multiple_of((2 * g + r) * SR, SR), SR)
        sk_r, sv_r = sk_ref[srows, :], sv_ref[srows, :]
        qrows = pl.ds(pl.multiple_of(r * QR, QR), QR)
        cached = coli < jnp.minimum(length, CP)
        for k in range(KVH):
            qk = jnp.concatenate([rxq[2 * k, qrows, :], rxq[2 * k + 1, qrows, :]], axis=0)
            cols = slice(k * HD, (k + 1) * HD)
            keys = jnp.concatenate([kbuf[r, :, cols], sk_r, pad], axis=0)
            vals = jnp.concatenate([vbuf[r, :, cols], sv_r, pad], axis=0)
            live = cached | (in_slots & (scol // 4 == k))
            s = dot_nt(qk, keys) * (HD**-0.5)
            s = jnp.where(live, s, -1e30)
            top = jnp.max(s, axis=-1, keepdims=True)
            e = jnp.where(live, jnp.exp(s - top), 0.0)
            p = (e / jnp.sum(e, axis=-1, keepdims=True)).astype(BF16)
            o = jnp.dot(p, vals, preferred_element_type=F32).astype(BF16)
            outb[2 * k, qrows, :] = o[:QR]
            outb[2 * k + 1, qrows, :] = o[QR:]
        return c

    lax.fori_loop(0, 2, attend, 0)

    def o_copy(j):
        dst = rem_mp(j)
        return remote(outb.at[dst], topb.at[g, m], o_s.at[j], o_r.at[m], at(mm=dst))

    def o_start(j, c):
        o_copy(j).start()
        return c

    lax.fori_loop(1, MP, o_start, 0)
    topb[g, m] = outb[m]

    s_reduce(0)

    def c_wait(b, c):
        src = half * g + b
        there = remote(cot_hbm, cbuf.at[b], c_s.at[b], c_r.at[b], at(mm=src))

        @pl.when(src != m)
        def _():
            there.wait_recv()

        return c

    lax.fori_loop(0, half, c_wait, 0)

    @pl.when(sends_cot)
    def _():
        own_cot.wait()

    remote(red.at[0, g], red.at[0, 1 - g], red_s.at[0], red_r.at[0], at(gg=1 - g)).wait_recv()

    def sums(ph, n):
        return jnp.concatenate([red[ph, 0, n : n + 1, :], red[ph, 1, n : n + 1, :]], axis=1)

    def inv(total):
        return lax.rsqrt(total * (1.0 / D) + EPS)

    def scale_cot(n, row):
        ax[n] = (cbuf[...].reshape(HC, T).astype(F32) * row).astype(BF16)

    scale = (2.0 * D) ** -0.5
    FB = min(F, 256)
    CB = min(HC, 256)

    scale_cot(0, inv(sums(0, 0)))

    def tiles(i, terms):
        def one(n, c):
            rows = pl.ds(pl.multiple_of((n % (HC // CB)) * CB, CB), CB)
            fb = n // (HC // CB)
            cols = pl.ds(pl.multiple_of(fb * FB, FB), FB)
            total = None
            for n_x, gain in terms:
                part = jnp.dot(ax[n_x, rows, :], vx[n_x, :, cols], preferred_element_type=F32)
                if gain is not None:
                    part = part * jg_ref[gain : gain + 1, cols]
                total = part if total is None else total + part
            tb[i, rows, cols] = (total * (ng_ref[i : i + 1, cols] * scale)).astype(BF16)
            return c

        lax.fori_loop(0, (HC // CB) * (F // FB), one, 0)

    FH = F // 2

    def zrows(zz):
        return pl.ds(pl.multiple_of(lax.rem(zz + NZ, NZ) * RB, RB), RB)

    def ring_cols(k, way):
        return slice(way * FH, (way + 1) * FH) if k == 1 else slice(0, F)

    def ring_copy(i, way, k):
        cols = ring_cols(k, way)
        step = 1 if way == 0 else -1
        if k == 1:
            src = tb.at[i, zrows(z + step * H), cols]
        else:
            src = sring.at[i, way, k - 2]
        dst = rring.at[i, way, k - 1, :, cols]
        return remote(src, dst, ring_s.at[i, way, k - 1], ring_r.at[i, way, k - 1], at(dd=zdev(z + step)))

    def ring_step(i, k):
        for way in range(2):
            if k > 1:
                step = 1 if way == 0 else -1
                ring_copy(i, way, k - 1).wait_recv()
                rows = zrows(z + step * (H + 1 - k))
                cols = ring_cols(k - 1, way)
                if k == 2:
                    sring[i, way, 0] = tb[i, rows, :]
                own = tb[i, rows, cols].astype(F32)
                sring[i, way, k - 2, :, cols] = (own + rring[i, way, k - 2, :, cols].astype(F32)).astype(BF16)
            ring_copy(i, way, k).start()

    def y_copy(i):
        return remote(sy.at[i], ry.at[i], y_s.at[i], y_r.at[i], at(dd=z * NY + 1 - y))

    def ring_end(i):
        for way in range(2):
            ring_copy(i, way, H).wait_recv()

        def total(yy):
            rows = pl.ds(pl.multiple_of(z * RB + yy * SH, SH), SH)
            here = pl.ds(pl.multiple_of(yy * SH, SH), SH)
            t = tb[i, rows, :].astype(F32)
            if H > 1:
                for way in range(2):
                    t = t + rring[i, way, H - 1, here, :].astype(F32)
            else:
                t = t + jnp.concatenate(
                    [rring[i, way, 0, here, ring_cols(1, way)].astype(F32) for way in range(2)], axis=1
                )
            return t

        if NY == 2:
            sy[i] = total(1 - y).astype(BF16)
            y_copy(i).start()
        return total(y)

    def grad_end(i, t):
        if NY == 2:
            y_copy(i).wait_recv()
            t = t + ry[i].astype(F32)
        return t.reshape(SH, LT, HD).reshape(SH * LT, HD)

    def gain_part(i, grad):
        w = wbuf[pl.ds(i, SH * LT, stride=2), :].astype(BF16).astype(F32)
        part = jnp.sum((w * grad).reshape(SH, LT, HD), axis=0)
        gs1[pl.ds(i * LT, LT), :] = part / ngn_ref[pl.ds(i, LT, stride=2), :]

    def adam(i, grad):
        rows = pl.ds(i, SH * LT, stride=2)
        w = wbuf[rows, :]
        a = first_beta * m1buf[rows, :] + (1.0 - first_beta) * grad
        b = second_beta * m2buf[rows, :] + (1.0 - second_beta) * grad * grad
        m1_out[rows, :] = a
        m2_out[rows, :] = b
        ca = a * (1.0 / (1.0 - first_beta**adam_steps))
        cb = b * (1.0 / (1.0 - second_beta**adam_steps))
        w_out[rows, :] = w - learn_rate * (ca / (jnp.sqrt(cb) + 1e-08) + decay_rate * w)

    tiles(0, ((0, None),))
    ring_step(0, 1)

    for gg in range(2):
        relayout_all(1, lambda i, gg: lob[i, gg], gg)
        relayout_all(2, lambda i, gg: mib[i, gg], gg)

    def o_wait(j, c):
        src = rem_mp(j)
        remote(outb.at[src], topb.at[g, src], o_s.at[j], o_r.at[src], at(mm=src)).wait_recv()
        return c

    lax.fori_loop(1, MP, o_wait, 0)
    top_copy = remote(topb.at[g], topb.at[g], top_s, top_r, at(gg=1 - g))
    top_copy.start()

    def stats1(i, c):
        l = native_block(lob[i, g], i)
        v = native_block(mib[i, g], i)
        t = native_block(topb[g, i], i)
        gl, gv, gt = l * g0, v * g1, t * g2
        rows = pl.ds(pl.multiple_of(i * SUB, SUB), SUB)
        for n, p in enumerate((t * t, gt * gt, gl * gt, gv * gt)):
            zbuf[n, rows, :] = fold(p)
        return c

    lax.fori_loop(0, MP, stats1, 0)
    s_begin(1, 4)
    if H >= 2:
        ring_step(0, 2)
    relayout_all(3, lambda i, gg: topb[gg, i], g)
    s_reduce(1)
    if H >= 3:
        ring_step(0, 3)
    remote(topb.at[g], topb.at[1 - g], top_s, top_r, at(gg=1 - g)).wait_recv()
    relayout_all(3, lambda i, gg: topb[gg, i], 1 - g)
    remote(red.at[1, g], red.at[1, 1 - g], red_s.at[1], red_r.at[1], at(gg=1 - g)).wait_recv()
    rl, rv, rt = inv(sums(0, 1)), inv(sums(0, 2)), inv(sums(1, 0))
    joined = (
        rl * rl * sums(0, 3)
        + rv * rv * sums(0, 4)
        + rt * rt * sums(1, 1)
        + 2.0 * (rl * rv * sums(0, 5) + rl * rt * sums(1, 2) + rv * rt * sums(1, 3))
    )
    rj = inv(jnp.maximum(joined, 0.0))
    scale_cot(1, rl * rj)
    scale_cot(2, rv * rj)
    scale_cot(3, rt * rj)
    tiles(1, ((1, 0), (2, 1), (3, 2)))
    ring_step(1, 1)
    if H >= 4:
        ring_step(0, 4)
    if H >= 2:
        ring_step(1, 2)
    part0 = ring_end(0)
    if H >= 3:
        ring_step(1, 3)
    loads["w"].wait()
    loads["m1"].wait()
    loads["m2"].wait()
    grad0 = grad_end(0, part0)
    gain_part(0, grad0)
    adam(0, grad0)
    if H >= 4:
        ring_step(1, 4)
    grad1 = grad_end(1, ring_end(1))
    gain_part(1, grad1)

    pairs = [(1 - g, z * NY + y)]
    if NY == 2:
        pairs += [(g, z * NY + 1 - y), (1 - g, z * NY + 1 - y)]
    g1_copies = [
        remote(gs1, gr1.at[n], g1_s.at[n], g1_r.at[n], at(gg=gg, dd=dd)) for n, (gg, dd) in enumerate(pairs)
    ]
    for copy in g1_copies:
        copy.start()
    adam(1, grad1)
    total = gs1[...]
    for n, copy in enumerate(g1_copies):
        copy.wait_recv()
        total = total + gr1[n]
    gs2[...] = total

    def g2_copy(j):
        return remote(gs2, gr2.at[z], g2_s.at[j], g2_r.at[z], at(dd=zdev(z + j)))

    for j in range(1, NZ):
        g2_copy(j).start()
    for j in range(1, NZ):
        src = lax.rem(z + j, NZ)
        remote(gs2, gr2.at[src], g2_s.at[j], g2_r.at[src], at(dd=zdev(z + j))).wait_recv()
        total = total + gr2[src]
    gain_out[pl.ds(0, LT, stride=2), :] = total[:LT]
    gain_out[pl.ds(1, LT, stride=2), :] = total[LT:]

    def drain(j, c):
        q_copy(j).wait_send()
        o_copy(j).wait_send()
        s_copy(0, j).wait_send()
        s_copy(1, j).wait_send()
        return c

    lax.fori_loop(1, MP, drain, 0)

    @pl.when(sends_cot)
    def _():
        def c_drain(j, c):
            c_copy(j).wait_send()
            return c

        lax.fori_loop(1, MP, c_drain, 0)

    for ph in range(2):
        red_copy(ph).wait_send()
    top_copy.wait_send()
    for i in range(2):
        for way in range(2):
            for k in range(1, H + 1):
                ring_copy(i, way, k).wait_send()
        if NY == 2:
            y_copy(i).wait_send()
    for copy in g1_copies:
        copy.wait_send()
    for j in range(1, NZ):
        g2_copy(j).wait_send()


def shards(
    NZ, NY, MP,
    queries, cache_keys, cache_values, slot_keys, slot_values, cache_lengths,
    embeddings, layer_low, layer_mid, accepted, join_gain, norm_gain,
    key_cotangent, key_weight, moment_first, moment_second,
):
    rows, slots, F = embeddings.shape
    D = F * MP
    KW = cache_keys.shape[2]
    KVH = KW // HD
    SH = key_weight.shape[0]
    HC = SH * NZ * NY
    T = rows * slots
    TH = T // 2
    LT = F // HD
    RB = NY * SH
    H = NZ // 2
    slot_index = jnp.arange(slots, dtype=jnp.int32)
    weight = jnp.where(
        slot_index[None, :] < accepted[:, None],
        jnp.float32(slot_decay) ** slot_index.astype(F32)[None, :],
        0.0,
    )
    scaled = (weight[:, :, None] * key_cotangent.astype(F32)).astype(BF16)
    cols = scaled.shape[2]
    scaled = scaled.reshape(MP, 2, 2, slots, cols).transpose(4, 1, 0, 2, 3).reshape(cols, T)

    def tokens(x):
        return native(x).reshape(MP, 2, 2 * LT * slots, HD)

    hbm = pl.BlockSpec(memory_space=pl.ANY)
    vmem = pl.BlockSpec(memory_space=pltpu.VMEM)
    smem = pl.BlockSpec(memory_space=pltpu.SMEM)
    dma = pltpu.SemaphoreType.DMA
    B = 2 * LT * slots
    shape = jax.ShapeDtypeStruct
    outs = pl.pallas_call(
        functools.partial(kernel, (NZ, NY, MP, KVH, F, D, HC, SH)),
        out_shape=(
            shape((SH * 2 * LT, HD), F32),
            shape((SH * 2 * LT, HD), F32),
            shape((SH * 2 * LT, HD), F32),
            shape((2 * LT, HD), F32),
        ),
        in_specs=[hbm, hbm, hbm, vmem, vmem, smem, hbm, hbm, hbm, hbm, vmem, vmem, vmem, hbm, hbm, hbm],
        out_specs=(vmem, vmem, vmem, vmem),
        scratch_shapes=[
            pltpu.VMEM((MP, B, HD), BF16),
            pltpu.VMEM((2, 64, KW), BF16),
            pltpu.VMEM((2, 64, KW), BF16),
            pltpu.VMEM((MP, B, HD), BF16),
            pltpu.VMEM((MP, 2, B, HD), BF16),
            pltpu.VMEM((MP, 2, B, HD), BF16),
            pltpu.VMEM((MP, 2, B, HD), BF16),
            pltpu.VMEM((2, MP, B, HD), BF16),
            pltpu.VMEM((MP // 2, cols, T), BF16),
            pltpu.VMEM((SH * 2 * LT, HD), F32),
            pltpu.VMEM((SH * 2 * LT, HD), F32),
            pltpu.VMEM((SH * 2 * LT, HD), F32),
            pltpu.VMEM((3, LT // 2, SUB, HD), F32),
            pltpu.VMEM((SUB, TH, HD), F32),
            pltpu.VMEM((2, SUB, TH), F32),
            pltpu.VMEM((2, MP, SUB, TH), F32),
            pltpu.VMEM((2, 2, SUB, TH), F32),
            pltpu.VMEM((4, T, F), BF16),
            pltpu.VMEM((4, HC, T), BF16),
            pltpu.VMEM((2, HC, F), BF16),
            pltpu.VMEM((2, 2, max(H - 1, 1), RB, F), BF16),
            pltpu.VMEM((2, 2, H, RB, F), BF16),
            pltpu.VMEM((2, SH, F), BF16),
            pltpu.VMEM((2, SH, F), BF16),
            pltpu.VMEM((2 * LT, HD), F32),
            pltpu.VMEM((3, 2 * LT, HD), F32),
            pltpu.VMEM((2 * LT, HD), F32),
            pltpu.VMEM((NZ, 2 * LT, HD), F32),
            dma((9,)),
            dma((MP,)), dma((MP,)),
            dma((MP,)), dma((MP // 2,)),
            dma((MP,)), dma((MP,)),
            dma((2, MP)), dma((2, MP)),
            dma((2,)), dma((2,)),
            dma, dma,
            dma((2, 2, H)), dma((2, 2, H)),
            dma((2,)), dma((2,)),
            dma((3,)), dma((3,)),
            dma((NZ,)), dma((NZ,)),
        ],
        compiler_params=pltpu.CompilerParams(
            collective_id=0, has_side_effects=True, vmem_limit_bytes=48 * 1024 * 1024
        ),
        cost_estimate=pl.CostEstimate(
            flops=2 * 4 * HC * T * F, bytes_accessed=6 * 1024 * 1024, transcendentals=0
        ),
        name="draft_step",
    )(
        tokens(queries), cache_keys, cache_values, native(slot_keys), native(slot_values), cache_lengths,
        tokens(embeddings), tokens(layer_low), tokens(layer_mid), scaled,
        join_gain, norm_gain, native(norm_gain[None]),
        native(key_weight), native(moment_first), native(moment_second),
    )
    new = [from_native(x, SH, 2, F) for x in outs[:3]]
    return (*new, from_native(outs[3], 1, 2, F)[0])


def solution(mesh, NY=2):
    NZ, MP = mesh.shape["dp"] // NY, mesh.shape["mp"]
    tokens, owners, moments = P("dp", None, "mp"), P(("dp", "mp"), None, None), P(("group", "dp"), None, "mp")
    return jax.shard_map(
        functools.partial(shards, NZ, NY, MP),
        mesh=mesh,
        in_specs=(
            tokens, owners, owners, owners, owners, P(("dp", "mp")), tokens, tokens, tokens, P("dp"),
            P(None, "mp"), P(None, "mp"), tokens, moments, moments, moments,
        ),
        out_specs=(moments, moments, moments, P(None, "mp")),
        check_vma=False,
    )
```

time: 656 us -> 98.3 us (0.15)
  waiting for transfers between devices: 284 us -> 0 us
  blocking collectives: 193 us -> 0 us
  local copies, waits for them, and re-layouts: 127 us -> 11.6 us
  Pallas kernels: 0 us -> 83.6 us
  starting transfers between devices: 15.9 us -> 0 us
  between operations: 14.3 us -> 0.74 us
  other arithmetic: 14.5 us -> 1.75 us
    reduce_scatter x1 -> x0, waiting for transfers between devices: 158 us -> none  [shards(): lax.psum_scatter(lax.cond(trainer, compute_term, lambda: jnp.zeros((row_c...]
    psum x3 -> x0, blocking collectives: 151 us -> none  [the longest x1 86.6 us: shards(): gain_grad = lax.psum(local_gain, ('group', 'dp'))]
    all_gather x1 -> x0, waiting for transfers between devices: 99.8 us -> none  [shards(): lax.all_gather(weight_copy, ('group', 'dp'), axis=0, tiled=True)]
    pallas_call x0 -> x1, Pallas kernels: none -> 83.6 us  [shards(): pl.pallas_call(functools.partial(kernel, (NZ, NY, MP, KVH, F, D, HC, SH))...]
    unnamed x30 -> x32, local copies, waits for them, and re-layouts: 70.8 us -> 11.5 us
    all_gather x1 -> x0, blocking collectives: 42.2 us -> none  [shards(): cotangent = lax.all_gather(key_cotangent, 'mp', axis=2, tiled=True)]
    all_to_all x1 -> x0, local copies, waits for them, and re-layouts: 24.7 us -> none  [shards(): lax.all_to_all(attended, 'mp', split_axis=2, concat_axis=0, tiled=True)]
    cond x3 -> x0, local copies, waits for them, and re-layouts: 20.1 us -> none  [the longest x1 16.2 us: shards(): lax.cond(serving, lambda: attend_rows(local_queries, cache_keys, cache_va...]
  transfers between devices with their start and end apart: 5 -> 0, of which waited for: 4 -> 0; matrix products, arithmetic and copies ran while one was open for 2% -> 0% of each run, Pallas kernels for 0% -> 0%
where the time goes in v1:
time: 98.3 us; the launch traced here: 97.7 us
  Pallas kernels  83.6 us (85%)
  local copies, waits for them, and re-layouts  11.6 us (12%)
  other arithmetic  1.75 us (2%)
    pallas_call x1, Pallas kernels, shards(): pl.pallas_call(functools.partial(kernel, (NZ, NY, MP, KVH, F, D, HC, SH))...  83.6 us
    unnamed x32, local copies, waits for them, and re-layouts  11.5 us

profile of v1, /device:TPU:1, one launch (start us, length us, event | category | flops | bytes accessed | tf_op | source)
XLA Modules:
  0.0 97.7 jit_solution(8170364970120131545)
XLA Ops:
  0.6 0.0 copy-start.6
  0.7 0.8 fusion
  1.4 1.0 multiply_convert_fusion
  2.4 0.0 copy-start.9
  2.4 0.0 copy-start.10
  2.5 0.0 copy-start.11
  2.5 0.0 copy-start.12
  2.5 0.0 copy-start.13
  2.5 0.1 copy.46.cot_hbm
  2.6 0.0 copy-done.6
  2.6 0.6 copy-done.9
  3.2 0.0 copy-done.10
  3.2 0.0 copy-done.11
  3.2 0.0 copy-done.12
  3.2 0.0 copy-done.13
  3.2 0.0 copy-start
  3.2 1.0 %copy-done = bf16[64,4,1024]{2,1,0:T(4,128)(2,1)S(1)} copy-done((bf16[64,4,1024]{2,1,0:T(4,128)(2,1)S(1)}, bf16[64,4,1024]{2,1,0:T(4,128)(2,1)}, u32[]{:S(2)}) %copy-start) | copy-done | bytes 524312
  4.3 0.0 copy-start.1
  4.3 1.0 %copy-done.1 = bf16[4,64,1024]{2,1,0:T(8,128)(2,1)S(1)} copy-done((bf16[4,64,1024]{2,1,0:T(8,128)(2,1)S(1)}, bf16[4,64,1024]{2,1,0:T(8,128)(2,1)}, u32[]{:S(2)}) %copy-start.1) | copy-done | bytes 524312
  5.3 0.0 copy-start.2
  5.3 1.0 %copy-done.2 = bf16[4,64,1024]{2,1,0:T(8,128)(2,1)S(1)} copy-done((bf16[4,64,1024]{2,1,0:T(8,128)(2,1)S(1)}, bf16[4,64,1024]{2,1,0:T(8,128)(2,1)}, u32[]{:S(2)}) %copy-start.2) | copy-done | bytes 524312
  6.3 0.0 copy-start.3
  6.4 1.0 %copy-done.3 = bf16[64,4,1024]{2,1,0:T(4,128)(2,1)S(1)} copy-done((bf16[64,4,1024]{2,1,0:T(4,128)(2,1)S(1)}, bf16[64,4,1024]{2,1,0:T(4,128)(2,1)}, u32[]{:S(2)}) %copy-start.3) | copy-done | bytes 524312
  7.4 0.0 copy-start.4
  7.4 1.0 %copy-done.4 = bf16[64,4,1024]{2,1,0:T(4,128)(2,1)S(1)} copy-done((bf16[64,4,1024]{2,1,0:T(4,128)(2,1)S(1)}, bf16[64,4,1024]{2,1,0:T(4,128)(2,1)}, u32[]{:S(2)}) %copy-start.4) | copy-done | bytes 524312
  8.4 0.0 copy-start.5
  8.4 1.0 %copy-done.5 = bf16[64,4,1024]{2,1,0:T(4,128)(2,1)S(1)} copy-done((bf16[64,4,1024]{2,1,0:T(4,128)(2,1)S(1)}, bf16[64,4,1024]{2,1,0:T(4,128)(2,1)}, u32[]{:S(2)}) %copy-start.5) | copy-done | bytes 524312
  9.5 0.0 copy-start.7
  9.5 0.9 copy-done.7
  10.4 0.0 copy-start.8
  10.4 0.9 copy-done.8
  11.4 83.6 %draft_step.1 = (f32[512,128]{1,0:T(8,128)S(1)}, f32[512,128]{1,0:T(8,128)S(1)}, f32[512,128]{1,0:T(8,128)S(1)}, f32[16,128]{1,0:T(8,128)S(1)}) custom-call(bf16[16,2,64,128]{3,2,1,0:T(8,128)(2,1)S(1)} %bitcast.74, bf16[4,64,1024]{2,1,0:T(8,128)(2,1)S(1)} %copy-done.1, bf16[4,64,1024]{2,1,0:T(8,128)(2,1)S(1)} %copy-done.2, bf16[128,128]{1,0:T(8,128)(2,1)S(1)} %bitcast.84, ...), custom_call_target="tpu_custom_call" | custom-call | flops 1073741824 | bytes 6291456 | tf_op jit(solution)/shard_map/draft_step/pallas_call | solution.py:581
  95.0 0.7 copy.55
  95.7 0.7 copy.56
  96.4 0.7 copy.57
  97.1 0.6 copy.58
  (2 shorter events, 0.0 us)
Async XLA Ops:
  0.6 2.0 %copy-start.6 = (f32[32,2,1024]{2,1,0:T(2,128)S(1)}, f32[32,2,1024]{2,1,0:T(2,128)}, u32[]{:S(2)}) copy-start(f32[32,2,1024]{2,1,0:T(2,128)} %param.29) | copy-start | bytes 786436
  2.4 0.8 copy-start.9
  2.4 0.8 copy-start.10
  2.5 0.8 copy-start.11
  2.5 0.7 copy-start.12
  2.5 0.7 copy-start.13
  3.2 1.0 %copy-start = (bf16[64,4,1024]{2,1,0:T(4,128)(2,1)S(1)}, bf16[64,4,1024]{2,1,0:T(4,128)(2,1)}, u32[]{:S(2)}) copy-start(bf16[64,4,1024]{2,1,0:T(4,128)(2,1)} %param.16) | copy-start | bytes 1572868
  4.3 1.0 %copy-start.1 = (bf16[4,64,1024]{2,1,0:T(8,128)(2,1)S(1)}, bf16[4,64,1024]{2,1,0:T(8,128)(2,1)}, u32[]{:S(2)}) copy-start(bf16[4,64,1024]{2,1,0:T(8,128)(2,1)} %ck_hbm.1) | copy-start | bytes 1572868
  5.3 1.0 %copy-start.2 = (bf16[4,64,1024]{2,1,0:T(8,128)(2,1)S(1)}, bf16[4,64,1024]{2,1,0:T(8,128)(2,1)}, u32[]{:S(2)}) copy-start(bf16[4,64,1024]{2,1,0:T(8,128)(2,1)} %cv_hbm.1) | copy-start | bytes 1572868
  6.3 1.0 %copy-start.3 = (bf16[64,4,1024]{2,1,0:T(4,128)(2,1)S(1)}, bf16[64,4,1024]{2,1,0:T(4,128)(2,1)}, u32[]{:S(2)}) copy-start(bf16[64,4,1024]{2,1,0:T(4,128)(2,1)} %param.22) | copy-start | bytes 1572868
  7.4 1.0 %copy-start.4 = (bf16[64,4,1024]{2,1,0:T(4,128)(2,1)S(1)}, bf16[64,4,1024]{2,1,0:T(4,128)(2,1)}, u32[]{:S(2)}) copy-start(bf16[64,4,1024]{2,1,0:T(4,128)(2,1)} %param.23) | copy-start | bytes 1572868
  8.4 1.0 %copy-start.5 = (bf16[64,4,1024]{2,1,0:T(4,128)(2,1)S(1)}, bf16[64,4,1024]{2,1,0:T(4,128)(2,1)}, u32[]{:S(2)}) copy-start(bf16[64,4,1024]{2,1,0:T(4,128)(2,1)} %param.24) | copy-start | bytes 1572868
  9.5 0.9 copy-start.7
  10.4 0.9 copy-start.8

commit v2 on v1

v2 whole, which is shorter than its diff:
```python
import functools

import jax
import jax.numpy as jnp
from jax import lax
from jax.experimental import pallas as pl
from jax.experimental.pallas import tpu as pltpu
from jax.sharding import PartitionSpec as P

HD = 128
SUB = 8
VMEM_BYTES = 62 * 1024 * 1024
NQ = 4
EPS = 1e-05
first_beta = 0.9
second_beta = 0.95
learn_rate = 0.05
decay_rate = 0.1
adam_steps = 3
slot_decay = 0.8
MESH = pl.DeviceIdType.MESH
F32 = jnp.float32
BF16 = jnp.bfloat16


def native(x):
    rows, slots, width = x.shape
    x = x.reshape(rows, slots, width // HD, HD).transpose(0, 2, 1, 3)
    return x.reshape(rows * (width // HD) * slots, HD)


def from_native(y, rows, slots, width):
    y = y.reshape(rows, width // HD, slots, HD).transpose(0, 2, 1, 3)
    return y.reshape(rows, slots, width)


def dot_nt(a, b, **kw):
    return lax.dot_general(a, b, (((1,), (1,)), ((), ())), preferred_element_type=F32, **kw)


def swap_halves(x):
    return jnp.concatenate([x[:, 4:], x[:, :4]], axis=1)


def kernel(
    dims,
    q_hbm, ck_hbm, cv_hbm, sk_ref, sv_ref, len_ref, em_hbm, lo_hbm, mi_hbm, cot_ref, acc_ref,
    jg_ref, ng_ref, ngn_ref, w_hbm, m1_hbm, m2_hbm,
    w_out, m1_out, m2_out, gain_out,
    rxq, kbuf, vbuf, outb, emb, lob, mib, topb, csend, cbuf, wbuf, m1buf, m2buf,
    gpat, zbuf, ssend, srecv, red, vx, ax, tb, sring, rring, sy, ry, own_t,
    w_two, wsend, wpart, gsend, grecv, gsib_s, gsib_r,
    lsem, q_s, q_r, c_s, c_r, o_s, o_r, s_s, s_r, red_s, red_r, top_s, top_r,
    ring_s, ring_r, y_s, y_r, wx_s, wx_r, g_s, g_r, gx_s, gx_r,
):
    NZ, NY, MP, KVH, F, D, HC, SH = dims
    LT = F // HD
    T = MP * 4 * SUB // 2
    TH = T // 2
    H = NZ // 2
    DP = NZ * NY
    RB = NY * SH
    FQ = F // NQ
    g = lax.axis_index("group")
    d = lax.axis_index("dp")
    m = lax.axis_index("mp")
    z, y = d // NY, lax.rem(d, NY)

    def at(gg=None, dd=None, mm=None):
        return (g if gg is None else gg, d if dd is None else dd, m if mm is None else mm)

    def zdev(zz):
        return lax.rem(zz + NZ, NZ) * NY + y

    def remote(src, dst, s, r, dev):
        return pltpu.make_async_remote_copy(
            src_ref=src, dst_ref=dst, send_sem=s, recv_sem=r, device_id=dev, device_id_type=MESH
        )

    def flip(a, j, n):
        out, bit = 0, 1
        while bit < n:
            p, q = lax.rem(a // bit, 2), lax.rem(j // bit, 2)
            out = out + bit * (p + q - 2 * p * q)
            bit *= 2
        return out

    def peer(j):
        return flip(m, jnp.int32(j), MP)

    loads = {
        "lo": pltpu.make_async_copy(lo_hbm, lob, lsem.at[0]),
        "mi": pltpu.make_async_copy(mi_hbm, mib, lsem.at[1]),
        "em": pltpu.make_async_copy(em_hbm, emb, lsem.at[2]),
        "q": pltpu.make_async_copy(q_hbm.at[m, g], rxq.at[m], lsem.at[3]),
        "k": pltpu.make_async_copy(ck_hbm.at[pl.ds(2 * g, 2)], kbuf, lsem.at[4]),
        "v": pltpu.make_async_copy(cv_hbm.at[pl.ds(2 * g, 2)], vbuf, lsem.at[5]),
        "w": pltpu.make_async_copy(w_hbm, wbuf, lsem.at[6]),
        "m1": pltpu.make_async_copy(m1_hbm, m1buf, lsem.at[7]),
        "m2": pltpu.make_async_copy(m2_hbm, m2buf, lsem.at[8]),
    }
    for load in loads.values():
        load.start()

    bar = pltpu.get_barrier_semaphore()

    def greet_dp(j, c):
        pl.semaphore_signal(bar, inc=1, device_id=at(dd=lax.rem(d + j, DP)), device_id_type=MESH)
        return c

    lax.fori_loop(1, DP, greet_dp, 0)

    def greet_mp(j, c):
        pl.semaphore_signal(bar, inc=1, device_id=at(mm=peer(MP - j)), device_id_type=MESH)
        return c

    lax.fori_loop(1, MP, greet_mp, 0)
    pl.semaphore_signal(bar, inc=1, device_id=at(gg=1 - g), device_id_type=MESH)

    RD = 4 * MP
    ct = cot_ref[...].astype(F32).reshape(RD // 2, 2, 4, cot_ref.shape[2])
    ct = jnp.concatenate([ct[:, 0], ct[:, 1]], axis=1).reshape(MP, 2, SUB, cot_ref.shape[2])
    ct = jnp.concatenate([ct[:, 0], ct[:, 1]], axis=0).reshape(T, cot_ref.shape[2])
    token = lax.broadcasted_iota(jnp.int32, (RD, T), 1)
    quad = token // 4
    part = lax.rem(quad, RD // 2)
    row = (part // 2) * 4 + (quad // (RD // 2)) * 2 + lax.rem(part, 2)
    pick = (lax.broadcasted_iota(jnp.int32, (RD, T), 0) == row).astype(BF16)
    lengths = jnp.broadcast_to(acc_ref[...].astype(F32), (SUB, RD)).astype(BF16)
    taken = jnp.dot(lengths, pick, preferred_element_type=F32)[:1]
    slot = lax.rem(lax.broadcasted_iota(jnp.int32, (1, T), 1), 4)
    weight = jnp.zeros((1, T), F32)
    for s in range(4):
        weight = jnp.where((slot == s) & (taken > s + 0.5), jnp.float32(slot_decay**s), weight)
    csend[...] = (ct.T * weight).astype(BF16)

    sub8 = lax.broadcasted_iota(jnp.int32, (1, SUB, HD), 1) < 4
    for a in range(3):
        for lp in range(LT // 2):
            lower = jg_ref[a : a + 1, 2 * lp * HD : (2 * lp + 1) * HD]
            upper = jg_ref[a : a + 1, (2 * lp + 1) * HD : (2 * lp + 2) * HD]
            gpat[a, lp] = jnp.where(sub8[0], lower, upper)

    def native_block(x):
        return x.astype(F32).reshape(2, LT // 2, SUB, HD)

    def fold(p):
        t = jnp.sum(p, axis=1)
        t = t + swap_halves(t)
        return jnp.where(sub8[0], t[0], t[1])

    loads["lo"].wait()
    loads["mi"].wait()
    loads["em"].wait()
    g0, g1, g2 = gpat[0], gpat[1], gpat[2]

    def stats0(i, c):
        e, l, v = native_block(emb[i, g]), native_block(lob[i, g]), native_block(mib[i, g])
        gl, gv = l * g0, v * g1
        rows = pl.ds(pl.multiple_of(i * SUB, SUB), SUB)
        for n, p in enumerate((e * e, l * l, v * v, gl * gl, gv * gv, gl * gv)):
            zbuf[n, rows, :] = fold(p)
        return c

    lax.fori_loop(0, MP, stats0, 0)

    def row_sums(count):
        total = jnp.zeros((SUB, TH), F32)
        for n in range(count):
            pick = (lax.broadcasted_iota(jnp.int32, (SUB, HD), 0) == n).astype(F32)
            total = total + dot_nt(pick, zbuf[n], precision=lax.Precision.HIGHEST)
        return total

    ssend[0] = row_sums(6)

    def relayout(x):
        x = native_block(x)
        a, b = x[0], x[1]
        return jnp.where(sub8, a, swap_halves(b)), jnp.where(sub8, swap_halves(a), b)

    def relayout_all(n, load, gg):
        def two(i, c):
            parts = [relayout(load(2 * i + h, gg)) for h in range(2)]
            rows = pl.ds(pl.multiple_of(gg * TH + i * 2 * SUB, 2 * SUB), 2 * SUB)
            for lp in range(LT // 2):
                for k in range(2):
                    tile = jnp.concatenate([parts[0][k][lp], parts[1][k][lp]], axis=0)
                    lt = 2 * lp + k
                    vx[n, rows, lt * HD : (lt + 1) * HD] = tile.astype(BF16)
            return c

        lax.fori_loop(0, MP // 2, two, 0)

    for gg in range(2):
        relayout_all(0, lambda i, gg: emb[i, gg], gg)
    loads["w"].wait()
    for i in range(2):
        w = wbuf[pl.ds(i, SH * LT, stride=2), :].astype(BF16).astype(F32)
        w_two[i] = w.reshape(SH, LT, HD).reshape(SH, F)
    wsend[...] = w_two[1].astype(BF16)

    pl.semaphore_wait(bar, DP - 1 + MP - 1 + 1)

    def q_copy(j):
        dst = peer(j)
        return remote(q_hbm.at[dst, g], rxq.at[m], q_s.at[j], q_r.at[m], at(mm=dst))

    def q_start(j, c):
        q_copy(MP - j).start()
        return c

    lax.fori_loop(1, MP, q_start, 0)

    half = MP // 2
    mine = lax.rem(m, half)
    sends_cot = (m // half) == g

    def c_copy(j):
        return remote(csend, cbuf.at[mine], c_s.at[j], c_r.at[mine], at(mm=peer(j)))

    @pl.when(sends_cot)
    def _():
        cbuf[mine] = csend[...]

        def c_start(j, c):
            c_copy(MP - j).start()
            return c

        lax.fori_loop(1, MP, c_start, 0)

    def s_copy(ph, j):
        return remote(ssend.at[ph], srecv.at[ph, m], s_s.at[ph, j], s_r.at[ph, m], at(mm=peer(j)))

    def s_begin(ph):
        def go(j, c):
            s_copy(ph, MP - j).start()
            return c

        lax.fori_loop(1, MP, go, 0)

    s_begin(0)

    def red_copy(ph):
        return remote(red.at[ph, g], red.at[ph, g], red_s.at[ph], red_r.at[ph], at(gg=1 - g))

    def s_reduce(ph):
        def add(j, total):
            src = peer(j)
            remote(
                ssend.at[ph], srecv.at[ph, src], s_s.at[ph, j], s_r.at[ph, src], at(mm=src)
            ).wait_recv()
            return total + srecv[ph, src]

        red[ph, g] = lax.fori_loop(1, MP, add, ssend[ph])
        red_copy(ph).start()

    def w_copy():
        return remote(wsend, wpart, wx_s, wx_r, at(dd=z * NY + 1 - y))

    for gg in range(2):
        relayout_all(1, lambda i, gg: lob[i, gg], gg)
        relayout_all(2, lambda i, gg: mib[i, gg], gg)

    loads["k"].wait()
    loads["v"].wait()
    loads["q"].wait()
    CP = 64
    SR = KVH * 4
    QR = 32
    rowi = lax.broadcasted_iota(jnp.int32, (2 * QR, HD), 0)
    coli = lax.broadcasted_iota(jnp.int32, (2 * QR, HD), 1)
    scol = coli - CP
    in_slots = (scol >= 0) & (scol < SR) & (lax.rem(scol, 4) <= lax.rem(rowi, 4))
    slot_head = scol // 4
    pad = jnp.zeros((HD - CP - SR, HD), BF16)
    slot_rows = [pl.ds(pl.multiple_of((2 * g + r) * SR, SR), SR) for r in range(2)]
    cached = [coli < jnp.minimum(len_ref[2 * g + r], CP) for r in range(2)]

    def o_copy(dst):
        return remote(outb.at[dst], topb.at[g, m], o_s.at[dst], o_r.at[m], at(mm=dst))

    def attend(j, c):
        k = flip(m // 2, j, KVH)
        for h in range(2):
            src = 2 * k + h

            @pl.when(src != m)
            def _():
                remote(q_hbm.at[src, g], rxq.at[src], q_s.at[src], q_r.at[src], at(mm=src)).wait_recv()

        cols = pl.ds(pl.multiple_of(k * HD, HD), HD)
        for r in range(2):
            qrows = slice(r * QR, (r + 1) * QR)
            qk = jnp.concatenate([rxq[2 * k, qrows, :], rxq[2 * k + 1, qrows, :]], axis=0)
            keys = jnp.concatenate([kbuf[r, :, cols], sk_ref[slot_rows[r], :], pad], axis=0)
            vals = jnp.concatenate([vbuf[r, :, cols], sv_ref[slot_rows[r], :], pad], axis=0)
            live = cached[r] | (in_slots & (slot_head == k))
            s = dot_nt(qk, keys) * (HD**-0.5)
            s = jnp.where(live, s, -1e30)
            top = jnp.max(s, axis=-1, keepdims=True)
            e = jnp.where(live, jnp.exp(s - top), 0.0)
            p = (e / jnp.sum(e, axis=-1, keepdims=True)).astype(BF16)
            o = jnp.dot(p, vals, preferred_element_type=F32).astype(BF16)
            outb[2 * k, qrows, :] = o[:QR]
            outb[2 * k + 1, qrows, :] = o[QR:]
        for h in range(2):
            dst = 2 * k + h

            @pl.when(dst != m)
            def _():
                o_copy(dst).start()

        return c

    lax.fori_loop(0, KVH, attend, 0)
    topb[g, m] = outb[m]

    s_reduce(0)

    def c_wait(b, c):
        src = half * g + b

        @pl.when(src != m)
        def _():
            remote(csend, cbuf.at[b], c_s.at[b], c_r.at[b], at(mm=src)).wait_recv()

        return c

    lax.fori_loop(0, half, c_wait, 0)
    remote(red.at[0, g], red.at[0, 1 - g], red_s.at[0], red_r.at[0], at(gg=1 - g)).wait_recv()

    def sums(ph, n):
        return jnp.concatenate([red[ph, 0, n : n + 1, :], red[ph, 1, n : n + 1, :]], axis=1)

    def inv(total):
        return lax.rsqrt(total * (1.0 / D) + EPS)

    def scale_cot(n, row):
        ax[n] = (cbuf[...].reshape(HC, T).astype(F32) * row).astype(BF16)

    scale = (2.0 * D) ** -0.5
    CB = min(HC, 256)

    def tile(i, q, terms):
        cols = slice(q * FQ, (q + 1) * FQ)

        def one(n, c):
            rows = pl.ds(pl.multiple_of(n * CB, CB), CB)
            total = None
            for n_x, gain in terms:
                part = jnp.dot(ax[n_x, rows, :], vx[n_x, :, cols], preferred_element_type=F32)
                if gain is not None:
                    part = part * jg_ref[gain : gain + 1, cols]
                total = part if total is None else total + part
            tb[i, q, rows, :] = (total * (ng_ref[i : i + 1, cols] * scale)).astype(BF16)
            return c

        lax.fori_loop(0, HC // CB, one, 0)

    ORDER = (0, 3, 1, 2)

    def length(way, q):
        return H if (way == 0) == (q < NQ // 2) else H - 1

    def zrows(zz):
        return pl.ds(pl.multiple_of(lax.rem(zz + NZ, NZ) * RB, RB), RB)

    def ring_copy(i, way, q, s):
        step = 1 if way == 0 else -1
        if s == 1:
            src = tb.at[i, q, zrows(z + step * length(way, q))]
        else:
            src = sring.at[i, way, q, s - 2]
        return remote(
            src, rring.at[i, way, q, s - 1], ring_s.at[i, way, q, s - 1], ring_r.at[i, way, q, s - 1],
            at(dd=zdev(z + step)),
        )

    def ring_step(i, s, q):
        for way in range(2):
            if s > length(way, q):
                continue
            if s > 1:
                ring_copy(i, way, q, s - 1).wait_recv()
                step = 1 if way == 0 else -1
                own = tb[i, q, zrows(z + step * (length(way, q) + 1 - s)), :].astype(F32)
                sring[i, way, q, s - 2] = (own + rring[i, way, q, s - 2].astype(F32)).astype(BF16)
            ring_copy(i, way, q, s).start()

    def ring_steps(i, s):
        for q in ORDER:
            ring_step(i, s, q)

    def gradient(i, terms):
        for q in ORDER:
            tile(i, q, terms)
            ring_step(i, 1, q)

    def y_copy(i, q):
        return remote(sy.at[i, q], ry.at[i, q], y_s.at[i, q], y_r.at[i, q], at(dd=z * NY + 1 - y))

    def ring_end(i):
        for q in ORDER:
            for way in range(2):
                if length(way, q) > 0:
                    ring_copy(i, way, q, length(way, q)).wait_recv()
            cols = slice(q * FQ, (q + 1) * FQ)

            def total(yy):
                t = tb[i, q, pl.ds(pl.multiple_of(z * RB + yy * SH, SH), SH), :].astype(F32)
                for way in range(2):
                    if length(way, q) > 0:
                        here = pl.ds(pl.multiple_of(yy * SH, SH), SH)
                        t = t + rring[i, way, q, length(way, q) - 1, here, :].astype(F32)
                return t

            if NY == 2:
                other = total(1 - y)
                sy[i, q] = other.astype(BF16)
                y_copy(i, q).start()
            here = total(y)
            own_t[i, :, cols] = here
            if i == 1:
                part = here * w_two[1, :, cols]
                if NY == 2:
                    part = part + other * wpart[:, cols].astype(F32)
                w_two[0, 0:1, cols] = jnp.sum(part, axis=0, keepdims=True)

    def grad_end(i):
        for q in range(NQ):
            if NY == 2:
                cols = slice(q * FQ, (q + 1) * FQ)
                y_copy(i, q).wait_recv()
                own_t[i, :, cols] = own_t[i, :, cols] + ry[i, q].astype(F32)

    def g_copy(i, j):
        return remote(gsend.at[i], grecv.at[i, d], g_s.at[i, j], g_r.at[i, d], at(dd=lax.rem(d + j, DP)))

    def gain_send(i, row):
        tiles = jnp.concatenate([row[:, t * HD : (t + 1) * HD] for t in range(LT)], axis=0)
        gsend[i] = tiles / ngn_ref[pl.ds(i, LT, stride=2), :]

        def go(j, c):
            g_copy(i, j).start()
            return c

        lax.fori_loop(1, DP, go, 0)

    def gain_total(i):
        def add(j, total):
            src = lax.rem(d + j, DP)
            remote(gsend.at[i], grecv.at[i, src], g_s.at[i, j], g_r.at[i, src], at(dd=src)).wait_recv()
            return total + grecv[i, src]

        return lax.fori_loop(1, DP, add, gsend[i])

    def adam(i):
        rows = pl.ds(i, SH * LT, stride=2)
        grad = own_t[i].reshape(SH, LT, HD).reshape(SH * LT, HD)
        w = wbuf[rows, :]
        a = first_beta * m1buf[rows, :] + (1.0 - first_beta) * grad
        b = second_beta * m2buf[rows, :] + (1.0 - second_beta) * grad * grad
        m1_out[rows, :] = a
        m2_out[rows, :] = b
        ca = a * (1.0 / (1.0 - first_beta**adam_steps))
        cb = b * (1.0 / (1.0 - second_beta**adam_steps))
        w_out[rows, :] = w - learn_rate * (ca / (jnp.sqrt(cb) + 1e-08) + decay_rate * w)

    scale_cot(0, inv(sums(0, 0)))
    gradient(0, ((0, None),))

    def stats1(j, c):
        i = flip(m, j, MP)

        @pl.when(i != m)
        def _():
            remote(outb.at[i], topb.at[g, i], o_s.at[i], o_r.at[i], at(mm=i)).wait_recv()

        l, v, t = native_block(lob[i, g]), native_block(mib[i, g]), native_block(topb[g, i])
        gl, gv, gt = l * g0, v * g1, t * g2
        rows = pl.ds(pl.multiple_of(i * SUB, SUB), SUB)
        for n, p in enumerate((t * t, gt * gt, gl * gt, gv * gt)):
            zbuf[n, rows, :] = fold(p)
        return c

    lax.fori_loop(0, MP, stats1, 0)
    ssend[1] = row_sums(4)
    s_begin(1)
    top_copy = remote(topb.at[g], topb.at[g], top_s, top_r, at(gg=1 - g))
    top_copy.start()
    if NY == 2:
        w_copy().start()
    relayout_all(3, lambda i, gg: topb[gg, i], g)
    if H >= 2:
        ring_steps(0, 2)
    remote(topb.at[g], topb.at[1 - g], top_s, top_r, at(gg=1 - g)).wait_recv()
    relayout_all(3, lambda i, gg: topb[gg, i], 1 - g)
    if H >= 3:
        ring_steps(0, 3)
    s_reduce(1)
    remote(red.at[1, g], red.at[1, 1 - g], red_s.at[1], red_r.at[1], at(gg=1 - g)).wait_recv()

    rl, rv, rt = inv(sums(0, 1)), inv(sums(0, 2)), inv(sums(1, 0))
    joined = (
        rl * rl * sums(0, 3)
        + rv * rv * sums(0, 4)
        + rt * rt * sums(1, 1)
        + 2.0 * (rl * rv * sums(0, 5) + rl * rt * sums(1, 2) + rv * rt * sums(1, 3))
    )
    rj = inv(jnp.maximum(joined, 0.0))
    scale_cot(1, rl * rj)
    scale_cot(2, rv * rj)
    scale_cot(3, rt * rj)
    gradient(1, ((1, 0), (2, 1), (3, 2)))

    if H >= 4:
        ring_steps(0, 4)
    if H >= 2:
        ring_steps(1, 2)
    ring_end(0)
    if H >= 3:
        ring_steps(1, 3)
    loads["m1"].wait()
    loads["m2"].wait()
    grad_end(0)
    gain_send(0, jnp.sum(own_t[0] * w_two[0], axis=0, keepdims=True))
    adam(0)
    if NY == 2:
        w_copy().wait_recv()
    if H >= 4:
        ring_steps(1, 4)
    ring_end(1)
    gain_send(1, w_two[0, 0:1, :])
    grad_end(1)
    adam(1)

    for i in range(2):
        gsib_s[i] = gain_total(i)
    g_pair = remote(gsib_s, gsib_r, gx_s, gx_r, at(gg=1 - g))
    g_pair.start()
    g_pair.wait_recv()
    for i in range(2):
        gain_out[pl.ds(i, LT, stride=2), :] = gsib_s[i] + gsib_r[i]

    def drain(j, c):
        q_copy(j).wait_send()
        o_copy(peer(j)).wait_send()
        s_copy(0, j).wait_send()
        s_copy(1, j).wait_send()
        return c

    lax.fori_loop(1, MP, drain, 0)

    @pl.when(sends_cot)
    def _():
        def c_drain(j, c):
            c_copy(j).wait_send()
            return c

        lax.fori_loop(1, MP, c_drain, 0)

    for ph in range(2):
        red_copy(ph).wait_send()
    top_copy.wait_send()
    for i in range(2):
        for q in range(NQ):
            for way in range(2):
                for s in range(1, length(way, q) + 1):
                    ring_copy(i, way, q, s).wait_send()
            if NY == 2:
                y_copy(i, q).wait_send()

        def g_drain(j, c):
            g_copy(i, j).wait_send()
            return c

        lax.fori_loop(1, DP, g_drain, 0)
    if NY == 2:
        w_copy().wait_send()
    g_pair.wait_send()


def hand_on(*refs):
    n = len(refs) // 2
    sems = refs[-1]
    copies = [pltpu.make_async_copy(refs[i], refs[n + i], sems.at[i]) for i in range(n)]
    for copy in copies:
        copy.start()
    for copy in copies:
        copy.wait()


def shards(
    NZ, NY, MP,
    queries, cache_keys, cache_values, slot_keys, slot_values, cache_lengths,
    embeddings, layer_low, layer_mid, accepted, join_gain, norm_gain,
    key_cotangent, key_weight, moment_first, moment_second,
):
    rows, slots, F = embeddings.shape
    D = F * MP
    KW = cache_keys.shape[2]
    KVH = KW // HD
    SH = key_weight.shape[0]
    HC = SH * NZ * NY
    T = rows * slots
    TH = T // 2
    LT = F // HD
    RB = NY * SH
    H = NZ // 2
    cols = key_cotangent.shape[2]
    DP = NZ * NY
    FQ = F // NQ

    def tokens(x):
        return native(x).reshape(MP, 2, 2 * LT * slots, HD)

    hbm = pl.BlockSpec(memory_space=pl.ANY)
    vmem = pl.BlockSpec(memory_space=pltpu.VMEM)
    smem = pl.BlockSpec(memory_space=pltpu.SMEM)
    dma = pltpu.SemaphoreType.DMA
    B = 2 * LT * slots
    shape = jax.ShapeDtypeStruct
    outs = pl.pallas_call(
        functools.partial(kernel, (NZ, NY, MP, KVH, F, D, HC, SH)),
        out_shape=(
            shape((SH * 2 * LT, HD), F32),
            shape((SH * 2 * LT, HD), F32),
            shape((SH * 2 * LT, HD), F32),
            shape((2 * LT, HD), F32),
        ),
        in_specs=[hbm, hbm, hbm, vmem, vmem, smem, hbm, hbm, hbm] + [vmem] * 5 + [hbm, hbm, hbm],
        out_specs=(vmem, vmem, vmem, vmem),
        scratch_shapes=[
            pltpu.VMEM((MP, B, HD), BF16),
            pltpu.VMEM((2, 64, KW), BF16),
            pltpu.VMEM((2, 64, KW), BF16),
            pltpu.VMEM((MP, B, HD), BF16),
            pltpu.VMEM((MP, 2, B, HD), BF16),
            pltpu.VMEM((MP, 2, B, HD), BF16),
            pltpu.VMEM((MP, 2, B, HD), BF16),
            pltpu.VMEM((2, MP, B, HD), BF16),
            pltpu.VMEM((cols, T), BF16),
            pltpu.VMEM((MP // 2, cols, T), BF16),
            pltpu.VMEM((SH * 2 * LT, HD), F32),
            pltpu.VMEM((SH * 2 * LT, HD), F32),
            pltpu.VMEM((SH * 2 * LT, HD), F32),
            pltpu.VMEM((3, LT // 2, SUB, HD), F32),
            pltpu.VMEM((SUB, TH, HD), F32),
            pltpu.VMEM((2, SUB, TH), F32),
            pltpu.VMEM((2, MP, SUB, TH), F32),
            pltpu.VMEM((2, 2, SUB, TH), F32),
            pltpu.VMEM((4, T, F), BF16),
            pltpu.VMEM((4, HC, T), BF16),
            pltpu.VMEM((2, NQ, HC, FQ), BF16),
            pltpu.VMEM((2, 2, NQ, max(H - 1, 1), RB, FQ), BF16),
            pltpu.VMEM((2, 2, NQ, H, RB, FQ), BF16),
            pltpu.VMEM((2, NQ, SH, FQ), BF16),
            pltpu.VMEM((2, NQ, SH, FQ), BF16),
            pltpu.VMEM((2, SH, F), F32),
            pltpu.VMEM((2, SH, F), F32),
            pltpu.VMEM((SH, F), BF16),
            pltpu.VMEM((SH, F), BF16),
            pltpu.VMEM((2, LT, HD), F32),
            pltpu.VMEM((2, DP, LT, HD), F32),
            pltpu.VMEM((2, LT, HD), F32),
            pltpu.VMEM((2, LT, HD), F32),
            dma((9,)),
            dma((MP,)), dma((MP,)),
            dma((MP,)), dma((MP // 2,)),
            dma((MP,)), dma((MP,)),
            dma((2, MP)), dma((2, MP)),
            dma((2,)), dma((2,)),
            dma, dma,
            dma((2, 2, NQ, H)), dma((2, 2, NQ, H)),
            dma((2, NQ)), dma((2, NQ)),
            dma, dma,
            dma((2, DP)), dma((2, DP)),
            dma, dma,
        ],
        compiler_params=pltpu.CompilerParams(
            collective_id=0, has_side_effects=True, vmem_limit_bytes=VMEM_BYTES
        ),
        cost_estimate=pl.CostEstimate(
            flops=2 * 4 * HC * T * F, bytes_accessed=6 * 1024 * 1024, transcendentals=0
        ),
        name="draft_step",
    )(
        tokens(queries), cache_keys, cache_values, native(slot_keys), native(slot_values), cache_lengths,
        tokens(embeddings), tokens(layer_low), tokens(layer_mid), key_cotangent, accepted[None],
        join_gain, norm_gain, native(norm_gain[None]),
        native(key_weight), native(moment_first), native(moment_second),
    )
    outs = pl.pallas_call(
        hand_on,
        out_shape=[shape(x.shape, x.dtype) for x in outs],
        in_specs=[hbm] * 4,
        out_specs=[hbm] * 4,
        scratch_shapes=[dma((4,))],
        compiler_params=pltpu.CompilerParams(vmem_limit_bytes=VMEM_BYTES),
        name="hand_on",
    )(*outs)
    new = [from_native(x, SH, 2, F) for x in outs[:3]]
    return (*new, from_native(outs[3], 1, 2, F)[0])


def solution(mesh, NY=2):
    NZ, MP = mesh.shape["dp"] // NY, mesh.shape["mp"]
    tokens, owners, moments = P("dp", None, "mp"), P(("dp", "mp"), None, None), P(("group", "dp"), None, "mp")
    return jax.shard_map(
        functools.partial(shards, NZ, NY, MP),
        mesh=mesh,
        in_specs=(
            tokens, owners, owners, owners, owners, P(("dp", "mp")), tokens, tokens, tokens, P("dp"),
            P(None, "mp"), P(None, "mp"), tokens, moments, moments, moments,
        ),
        out_specs=(moments, moments, moments, P(None, "mp")),
        check_vma=False,
    )
```

time: 98.3 us -> 109 us (1.11)
  Pallas kernels: 83.6 us -> 108 us
  local copies, waits for them, and re-layouts: 11.6 us -> 0 us
  other arithmetic: 1.75 us -> 0 us
    pallas_call x0 -> x1, Pallas kernels: none -> 25.2 us  [shards(): pl.pallas_call(hand_on, out_shape=[shape(x.shape, x.dtype) for x in outs]...]
    unnamed x32 -> x0, local copies, waits for them, and re-layouts: 11.5 us -> none
where the time goes in v2:
time: 109 us; the launch traced here: 108 us
  Pallas kernels  108 us (99%)
    pallas_call x1, Pallas kernels, shards(): pl.pallas_call(functools.partial(kernel, (NZ, NY, MP, KVH, F, D, HC, SH))...  82.5 us
    pallas_call x1, Pallas kernels, shards(): pl.pallas_call(hand_on, out_shape=[shape(x.shape, x.dtype) for x in outs]...  25.2 us

profile of v2, /device:TPU:1, one launch (start us, length us, event | category | flops | bytes accessed | tf_op | source)
XLA Modules:
  0.0 108.4 jit_solution(11866300747531215359)
XLA Ops:
  0.6 82.5 %draft_step.1 = (f32[512,128]{1,0:T(8,128)}, f32[512,128]{1,0:T(8,128)}, f32[512,128]{1,0:T(8,128)}, f32[16,128]{1,0:T(8,128)}) custom-call(bf16[16,2,64,128]{3,2,1,0:T(8,128)(2,1)} %bitcast.71, bf16[4,64,1024]{2,1,0:T(8,128)(2,1)} %ck_hbm.1, bf16[4,64,1024]{2,1,0:T(8,128)(2,1)} %cv_hbm.1, bf16[128,128]{1,0:T(8,128)(2,1)} %bitcast.78, ...), custom_call_target="tpu_custom_call" | custom-call | flops 1073741824 | bytes 6291456 | tf_op jit(solution)/shard_map/draft_step/pallas_call | solution.py:623
  83.2 25.2 %hand_on.1 = (f32[512,128]{1,0:T(8,128)}, f32[512,128]{1,0:T(8,128)}, f32[512,128]{1,0:T(8,128)}, f32[16,128]{1,0:T(8,128)}) custom-call(f32[512,128]{1,0:T(8,128)} %get-tuple-element.12.refs_0_, f32[512,128]{1,0:T(8,128)} %get-tuple-element.13.refs_1_, f32[512,128]{1,0:T(8,128)} %get-tuple-element.14.refs_2_, f32[16,128]{1,0:T(8,128)} %get-tuple-element.15.refs_3_), custom_call_target="tpu_custom_call" | custom-call | tf_op jit(solution)/shard_map/hand_on/pallas_call | solution.py:693

commit v3 on v2

--- a/solution.py
+++ b/solution.py
@@ -50,21 +50,23 @@
     rxq, kbuf, vbuf, outb, emb, lob, mib, topb, csend, cbuf, wbuf, m1buf, m2buf,
     gpat, zbuf, ssend, srecv, red, vx, ax, tb, sring, rring, sy, ry, own_t,
     w_two, wsend, wpart, gsend, grecv, gsib_s, gsib_r,
-    lsem, q_s, q_r, c_s, c_r, o_s, o_r, s_s, s_r, red_s, red_r, top_s, top_r,
+    lsem, q_s, q_r, c_s, c_r, c2_s, c2_r, o_s, o_r, s_s, s_r, red_s, red_r, top_s, top_r,
     ring_s, ring_r, y_s, y_r, wx_s, wx_r, g_s, g_r, gx_s, gx_r,
 ):
-    NZ, NY, MP, KVH, F, D, HC, SH = dims
+    NZ, NY, MP, MX, KVH, F, D, HC, SH = dims
+    MY = MP // MX
+    YH = MY // 2
     LT = F // HD
     T = MP * 4 * SUB // 2
     TH = T // 2
     H = NZ // 2
     DP = NZ * NY
-    RB = NY * SH
-    FQ = F // NQ
+    FH = F // 2
     g = lax.axis_index("group")
     d = lax.axis_index("dp")
     m = lax.axis_index("mp")
     z, y = d // NY, lax.rem(d, NY)
+    ml, mx = m // MX, lax.rem(m, MX)
 
     def at(gg=None, dd=None, mm=None):
         return (g if gg is None else gg, d if dd is None else dd, m if mm is None else mm)
@@ -77,16 +79,22 @@
             src_ref=src, dst_ref=dst, send_sem=s, recv_sem=r, device_id=dev, device_id_type=MESH
         )
 
-    def flip(a, j, n):
-        out, bit = 0, 1
-        while bit < n:
-            p, q = lax.rem(a // bit, 2), lax.rem(j // bit, 2)
-            out = out + bit * (p + q - 2 * p * q)
-            bit *= 2
-        return out
+    def flips(a, n):
+        return [(b, b * (1 - 2 * lax.rem(a // b, 2))) for b in (1, 2, 4, 8) if b < n]
+
+    def flipped(a, bits, j):
+        for b, delta in bits:
+            if j & b:
+                a = a + delta
+        return a
+
+    m_bits, d_bits, x_bits, y_bits = flips(m, MP), flips(d, DP), flips(mx, MX), flips(ml, MY)
 
     def peer(j):
-        return flip(m, jnp.int32(j), MP)
+        return flipped(m, m_bits, j)
+
+    def dpeer(j):
+        return flipped(d, d_bits, j)
 
     loads = {
         "lo": pltpu.make_async_copy(lo_hbm, lob, lsem.at[0]),
@@ -104,17 +112,10 @@
 
     bar = pltpu.get_barrier_semaphore()
 
-    def greet_dp(j, c):
-        pl.semaphore_signal(bar, inc=1, device_id=at(dd=lax.rem(d + j, DP)), device_id_type=MESH)
-        return c
-
-    lax.fori_loop(1, DP, greet_dp, 0)
-
-    def greet_mp(j, c):
-        pl.semaphore_signal(bar, inc=1, device_id=at(mm=peer(MP - j)), device_id_type=MESH)
-        return c
-
-    lax.fori_loop(1, MP, greet_mp, 0)
+    for j in range(DP - 1, 0, -1):
+        pl.semaphore_signal(bar, inc=1, device_id=at(dd=dpeer(j)), device_id_type=MESH)
+    for j in range(MP - 1, 0, -1):
+        pl.semaphore_signal(bar, inc=1, device_id=at(mm=peer(j)), device_id_type=MESH)
     pl.semaphore_signal(bar, inc=1, device_id=at(gg=1 - g), device_id_type=MESH)
 
     RD = 4 * MP
@@ -203,55 +204,61 @@
 
     def q_copy(j):
         dst = peer(j)
-        return remote(q_hbm.at[dst, g], rxq.at[m], q_s.at[j], q_r.at[m], at(mm=dst))
-
-    def q_start(j, c):
-        q_copy(MP - j).start()
-        return c
-
-    lax.fori_loop(1, MP, q_start, 0)
-
-    half = MP // 2
-    mine = lax.rem(m, half)
-    sends_cot = (m // half) == g
+        return remote(q_hbm.at[dst, g], rxq.at[m], q_s, q_r.at[ml], at(mm=dst))
+
+    for j in range(MP - 1, 0, -1):
+        q_copy(j).start()
+
+    sends_cot = (ml // YH) == g
+    mine = lax.rem(ml, YH)
 
     def c_copy(j):
-        return remote(csend, cbuf.at[mine], c_s.at[j], c_r.at[mine], at(mm=peer(j)))
+        to = flipped(ml, y_bits, j) * MX + mx
+        return remote(csend, cbuf.at[mx, mine], c_s, c_r.at[mine], at(mm=to))
 
     @pl.when(sends_cot)
     def _():
-        cbuf[mine] = csend[...]
-
-        def c_start(j, c):
-            c_copy(MP - j).start()
-            return c
-
-        lax.fori_loop(1, MP, c_start, 0)
+        cbuf[mx, mine] = csend[...]
+        for j in range(MY - 1, 0, -1):
+            c_copy(j).start()
+
+    def c_forward(j):
+        to = ml * MX + flipped(mx, x_bits, j)
+        return remote(cbuf.at[mx], cbuf.at[mx], c2_s, c2_r, at(mm=to))
+
+    def c_turn():
+        for b in range(YH):
+
+            @pl.when((YH * g + b) != ml)
+            def _():
+                remote(csend, cbuf.at[mx, b], c_s, c_r.at[b], at(mm=(YH * g + b) * MX + mx)).wait_recv()
+
+        for j in range(MX - 1, 0, -1):
+            c_forward(j).start()
+
+    def c_end():
+        remote(cbuf.at[0 : MX - 1], cbuf.at[0 : MX - 1], c2_s, c2_r, at(mm=peer(1))).wait_recv()
 
     def s_copy(ph, j):
-        return remote(ssend.at[ph], srecv.at[ph, m], s_s.at[ph, j], s_r.at[ph, m], at(mm=peer(j)))
+        return remote(ssend.at[ph], srecv.at[ph, m], s_s.at[ph], s_r.at[ph], at(mm=peer(j)))
 
     def s_begin(ph):
-        def go(j, c):
-            s_copy(ph, MP - j).start()
-            return c
-
-        lax.fori_loop(1, MP, go, 0)
+        for j in range(MP - 1, 0, -1):
+            s_copy(ph, j).start()
+        srecv[ph, m] = ssend[ph]
 
     s_begin(0)
+
+    def s_all(ph):
+        some = srecv.at[ph, 0 : MP - 1]
+        return remote(some, some, s_s.at[ph], s_r.at[ph], at(mm=peer(1)))
 
     def red_copy(ph):
         return remote(red.at[ph, g], red.at[ph, g], red_s.at[ph], red_r.at[ph], at(gg=1 - g))
 
     def s_reduce(ph):
-        def add(j, total):
-            src = peer(j)
-            remote(
-                ssend.at[ph], srecv.at[ph, src], s_s.at[ph, j], s_r.at[ph, src], at(mm=src)
-            ).wait_recv()
-            return total + srecv[ph, src]
-
-        red[ph, g] = lax.fori_loop(1, MP, add, ssend[ph])
+        s_all(ph).wait_recv()
+        red[ph, g] = jnp.sum(srecv[ph], axis=0)
         red_copy(ph).start()
 
     def w_copy():
@@ -277,17 +284,9 @@
     cached = [coli < jnp.minimum(len_ref[2 * g + r], CP) for r in range(2)]
 
     def o_copy(dst):
-        return remote(outb.at[dst], topb.at[g, m], o_s.at[dst], o_r.at[m], at(mm=dst))
-
-    def attend(j, c):
-        k = flip(m // 2, j, KVH)
-        for h in range(2):
-            src = 2 * k + h
-
-            @pl.when(src != m)
-            def _():
-                remote(q_hbm.at[src, g], rxq.at[src], q_s.at[src], q_r.at[src], at(mm=src)).wait_recv()
-
+        return remote(outb.at[dst], topb.at[g, m], o_s, o_r.at[ml], at(mm=dst))
+
+    def attend(k):
         cols = pl.ds(pl.multiple_of(k * HD, HD), HD)
         for r in range(2):
             qrows = slice(r * QR, (r + 1) * QR)
@@ -301,32 +300,29 @@
             e = jnp.where(live, jnp.exp(s - top), 0.0)
             p = (e / jnp.sum(e, axis=-1, keepdims=True)).astype(BF16)
             o = jnp.dot(p, vals, preferred_element_type=F32).astype(BF16)
-            outb[2 * k, qrows, :] = o[:QR]
-            outb[2 * k + 1, qrows, :] = o[QR:]
-        for h in range(2):
-            dst = 2 * k + h
-
-            @pl.when(dst != m)
-            def _():
-                o_copy(dst).start()
-
-        return c
-
-    lax.fori_loop(0, KVH, attend, 0)
+            yield 2 * k, qrows, o[:QR]
+            yield 2 * k + 1, qrows, o[QR:]
+
+    for jy in range(MY):
+        yl = flipped(ml, y_bits, jy)
+        count = MX - 1 if jy == 0 else MX
+        some = rxq.at[0:count]
+        remote(some, some, q_s, q_r.at[yl], at(mm=peer(1))).wait_recv()
+        done = []
+        for h in range(MX // 2):
+            done += list(attend(yl * (MX // 2) + h))
+        for dst, qrows, o in done:
+            outb[dst, qrows, :] = o
+        for jx in range(MX):
+            if jx or jy:
+                o_copy(yl * MX + flipped(mx, x_bits, jx)).start()
+        if jy == min(1, MY - 1):
+            c_turn()
     topb[g, m] = outb[m]
 
     s_reduce(0)
 
-    def c_wait(b, c):
-        src = half * g + b
-
-        @pl.when(src != m)
-        def _():
-            remote(csend, cbuf.at[b], c_s.at[b], c_r.at[b], at(mm=src)).wait_recv()
-
-        return c
-
-    lax.fori_loop(0, half, c_wait, 0)
+    c_end()
     remote(red.at[0, g], red.at[0, 1 - g], red_s.at[0], red_r.at[0], at(gg=1 - g)).wait_recv()
 
     def sums(ph, n):
@@ -336,43 +332,47 @@
         return lax.rsqrt(total * (1.0 / D) + EPS)
 
     def scale_cot(n, row):
-        ax[n] = (cbuf[...].reshape(HC, T).astype(F32) * row).astype(BF16)
-
+        for b in range(YH):
+            for x in range(MX):
+                rows = slice((b * MX + x) * CW, (b * MX + x + 1) * CW)
+                ax[n, rows, :] = (cbuf[x, b].astype(F32) * row).astype(BF16)
+
+    CW = HC // (YH * MX)
     scale = (2.0 * D) ** -0.5
     CB = min(HC, 256)
+    ZB = CB // (NY * SH)
 
     def tile(i, q, terms):
-        cols = slice(q * FQ, (q + 1) * FQ)
-
-        def one(n, c):
-            rows = pl.ds(pl.multiple_of(n * CB, CB), CB)
+        cols = slice(q * FH // 2, (q + 1) * FH // 2)
+        here = slice((q % 2) * FH // 2, (q % 2 + 1) * FH // 2)
+        for n in range(HC // CB):
             total = None
             for n_x, gain in terms:
-                part = jnp.dot(ax[n_x, rows, :], vx[n_x, :, cols], preferred_element_type=F32)
+                part = jnp.dot(ax[n_x, n * CB : (n + 1) * CB, :], vx[n_x, :, cols], preferred_element_type=F32)
                 if gain is not None:
                     part = part * jg_ref[gain : gain + 1, cols]
                 total = part if total is None else total + part
-            tb[i, q, rows, :] = (total * (ng_ref[i : i + 1, cols] * scale)).astype(BF16)
-            return c
-
-        lax.fori_loop(0, HC // CB, one, 0)
-
-    ORDER = (0, 3, 1, 2)
+            total = (total * (ng_ref[i : i + 1, cols] * scale)).astype(BF16)
+            total = total.reshape(ZB, NY, SH, FH // 2)
+            for yy in range(NY):
+                tb[i, yy, q // 2, n * ZB : (n + 1) * ZB, :, here] = total[:, yy]
+
+    CHUNKS = [q for q in range(NQ) if NY == 2 or q >= 2]
+
+    def y_of(q):
+        return 1 - y if q < 2 else y
 
     def length(way, q):
-        return H if (way == 0) == (q < NQ // 2) else H - 1
-
-    def zrows(zz):
-        return pl.ds(pl.multiple_of(lax.rem(zz + NZ, NZ) * RB, RB), RB)
+        return H if (way == 0) == (q % 2 == 0) else H - 1
+
+    def term(i, q, zz):
+        return tb.at[i, y_of(q), q % 2, lax.rem(zz + NZ, NZ)]
 
     def ring_copy(i, way, q, s):
         step = 1 if way == 0 else -1
-        if s == 1:
-            src = tb.at[i, q, zrows(z + step * length(way, q))]
-        else:
-            src = sring.at[i, way, q, s - 2]
+        src = term(i, q, z + step * length(way, q)) if s == 1 else sring.at[i, way, q, s - 2]
         return remote(
-            src, rring.at[i, way, q, s - 1], ring_s.at[i, way, q, s - 1], ring_r.at[i, way, q, s - 1],
+            src, rring.at[i, way, q, s - 1], ring_s.at[i, int(s == H)], ring_r.at[i, way, q, s - 1],
             at(dd=zdev(z + step)),
         )
 
@@ -383,76 +383,84 @@
             if s > 1:
                 ring_copy(i, way, q, s - 1).wait_recv()
                 step = 1 if way == 0 else -1
-                own = tb[i, q, zrows(z + step * (length(way, q) + 1 - s)), :].astype(F32)
+                own = term(i, q, z + step * (length(way, q) + 1 - s))[...].astype(F32)
                 sring[i, way, q, s - 2] = (own + rring[i, way, q, s - 2].astype(F32)).astype(BF16)
             ring_copy(i, way, q, s).start()
 
     def ring_steps(i, s):
-        for q in ORDER:
+        for q in CHUNKS:
             ring_step(i, s, q)
 
+    def ring_sent(i):
+        ways = len(CHUNKS) // 2
+        if H > 1:
+            some = rring.at[i, :, 0 : len(CHUNKS), 0 : H - 1]
+            remote(some, some, ring_s.at[i, 0], ring_r.at[i, 0, 0, 0], at(dd=zdev(z + 1))).wait_send()
+        some = rring.at[i, :, 0:ways, 0]
+        remote(some, some, ring_s.at[i, 1], ring_r.at[i, 0, 0, 0], at(dd=zdev(z + 1))).wait_send()
+
     def gradient(i, terms):
-        for q in ORDER:
-            tile(i, q, terms)
-            ring_step(i, 1, q)
-
-    def y_copy(i, q):
-        return remote(sy.at[i, q], ry.at[i, q], y_s.at[i, q], y_r.at[i, q], at(dd=z * NY + 1 - y))
+        for ch in range(2):
+            tile(i, 2 * ch, terms)
+            tile(i, 2 * ch + 1, terms)
+            for q in CHUNKS:
+                if q % 2 == ch:
+                    ring_step(i, 1, q)
+
+    def y_copy(i, ch):
+        return remote(sy.at[i, ch], ry.at[i, ch], y_s.at[i], y_r.at[i, ch], at(dd=z * NY + 1 - y))
+
+    def y_sent(i):
+        remote(sy.at[i], ry.at[i], y_s.at[i], y_r.at[i, 0], at(dd=z * NY + 1 - y)).wait_send()
 
     def ring_end(i):
-        for q in ORDER:
+        gain = [None, None]
+        for q in CHUNKS:
+            ch = q % 2
+            cols = slice(ch * FH, (ch + 1) * FH)
+            t = term(i, q, z)[...].astype(F32)
             for way in range(2):
-                if length(way, q) > 0:
-                    ring_copy(i, way, q, length(way, q)).wait_recv()
-            cols = slice(q * FQ, (q + 1) * FQ)
-
-            def total(yy):
-                t = tb[i, q, pl.ds(pl.multiple_of(z * RB + yy * SH, SH), SH), :].astype(F32)
-                for way in range(2):
-                    if length(way, q) > 0:
-                        here = pl.ds(pl.multiple_of(yy * SH, SH), SH)
-                        t = t + rring[i, way, q, length(way, q) - 1, here, :].astype(F32)
-                return t
-
-            if NY == 2:
-                other = total(1 - y)
-                sy[i, q] = other.astype(BF16)
-                y_copy(i, q).start()
-            here = total(y)
-            own_t[i, :, cols] = here
-            if i == 1:
-                part = here * w_two[1, :, cols]
-                if NY == 2:
-                    part = part + other * wpart[:, cols].astype(F32)
-                w_two[0, 0:1, cols] = jnp.sum(part, axis=0, keepdims=True)
+                n = length(way, q)
+                if n > 0:
+                    ring_copy(i, way, q, n).wait_recv()
+                    t = t + rring[i, way, q, n - 1].astype(F32)
+            if q < 2:
+                sy[i, ch] = t.astype(BF16)
+                y_copy(i, ch).start()
+                if i == 1:
+                    gain[ch] = t * wpart[:, cols].astype(F32)
+            else:
+                own_t[i, :, cols] = t
+                if i == 1:
+                    part = t * w_two[1, :, cols]
+                    gain[ch] = part if gain[ch] is None else gain[ch] + part
+        if i == 1:
+            gain_send(1, jnp.sum(jnp.concatenate(gain, axis=1), axis=0, keepdims=True))
 
     def grad_end(i):
-        for q in range(NQ):
-            if NY == 2:
-                cols = slice(q * FQ, (q + 1) * FQ)
-                y_copy(i, q).wait_recv()
-                own_t[i, :, cols] = own_t[i, :, cols] + ry[i, q].astype(F32)
+        if NY == 2:
+            for ch in range(2):
+                cols = slice(ch * FH, (ch + 1) * FH)
+                y_copy(i, ch).wait_recv()
+                own_t[i, :, cols] = own_t[i, :, cols] + ry[i, ch].astype(F32)
 
     def g_copy(i, j):
-        return remote(gsend.at[i], grecv.at[i, d], g_s.at[i, j], g_r.at[i, d], at(dd=lax.rem(d + j, DP)))
+        return remote(gsend.at[i], grecv.at[i, d], g_s.at[i], g_r.at[i], at(dd=dpeer(j)))
 
     def gain_send(i, row):
         tiles = jnp.concatenate([row[:, t * HD : (t + 1) * HD] for t in range(LT)], axis=0)
         gsend[i] = tiles / ngn_ref[pl.ds(i, LT, stride=2), :]
-
-        def go(j, c):
+        for j in range(DP - 1, 0, -1):
             g_copy(i, j).start()
-            return c
-
-        lax.fori_loop(1, DP, go, 0)
+        grecv[i, d] = gsend[i]
+
+    def g_all(i):
+        some = grecv.at[i, 0 : DP - 1]
+        return remote(some, some, g_s.at[i], g_r.at[i], at(dd=dpeer(1)))
 
     def gain_total(i):
-        def add(j, total):
-            src = lax.rem(d + j, DP)
-            remote(gsend.at[i], grecv.at[i, src], g_s.at[i, j], g_r.at[i, src], at(dd=src)).wait_recv()
-            return total + grecv[i, src]
-
-        return lax.fori_loop(1, DP, add, gsend[i])
+        g_all(i).wait_recv()
+        return jnp.sum(grecv[i], axis=0)
 
     def adam(i):
         rows = pl.ds(i, SH * LT, stride=2)
@@ -469,21 +477,21 @@
     scale_cot(0, inv(sums(0, 0)))
     gradient(0, ((0, None),))
 
-    def stats1(j, c):
-        i = flip(m, j, MP)
-
-        @pl.when(i != m)
-        def _():
-            remote(outb.at[i], topb.at[g, i], o_s.at[i], o_r.at[i], at(mm=i)).wait_recv()
-
-        l, v, t = native_block(lob[i, g]), native_block(mib[i, g]), native_block(topb[g, i])
-        gl, gv, gt = l * g0, v * g1, t * g2
-        rows = pl.ds(pl.multiple_of(i * SUB, SUB), SUB)
-        for n, p in enumerate((t * t, gt * gt, gl * gt, gv * gt)):
-            zbuf[n, rows, :] = fold(p)
-        return c
-
-    lax.fori_loop(0, MP, stats1, 0)
+    for jy in range(MY):
+        yl = flipped(ml, y_bits, jy)
+        some = topb.at[0, 0 : MX - 1 if jy == 0 else MX]
+        remote(some, some, o_s, o_r.at[yl], at(mm=peer(1))).wait_recv()
+
+        def stats1(x, c):
+            i = yl * MX + x
+            l, v, t = native_block(lob[i, g]), native_block(mib[i, g]), native_block(topb[g, i])
+            gl, gv, gt = l * g0, v * g1, t * g2
+            rows = pl.ds(pl.multiple_of(i * SUB, SUB), SUB)
+            for n, p in enumerate((t * t, gt * gt, gl * gt, gv * gt)):
+                zbuf[n, rows, :] = fold(p)
+            return c
+
+        lax.fori_loop(0, MX, stats1, 0, unroll=2)
     ssend[1] = row_sums(4)
     s_begin(1)
     top_copy = remote(topb.at[g], topb.at[g], top_s, top_r, at(gg=1 - g))
@@ -497,6 +505,21 @@
     relayout_all(3, lambda i, gg: topb[gg, i], 1 - g)
     if H >= 3:
         ring_steps(0, 3)
+
+    def sent(block, count, sem, r):
+        some = block.at[0:count]
+        remote(some, some, sem, r, at(mm=peer(1))).wait_send()
+
+    sent(rxq, MP - 1, q_s, q_r.at[0])
+    sent(outb, MP - 1, o_s, o_r.at[0])
+    s_all(0).wait_send()
+    sent(cbuf, MX - 1, c2_s, c2_r)
+
+    @pl.when(sends_cot)
+    def _():
+        some = ax.at[0, 0 : (MY - 1) * CW]
+        remote(some, some, c_s, c_r.at[0], at(mm=peer(1))).wait_send()
+
     s_reduce(1)
     remote(red.at[1, g], red.at[1, 1 - g], red_s.at[1], red_r.at[1], at(gg=1 - g)).wait_recv()
 
@@ -530,7 +553,6 @@
     if H >= 4:
         ring_steps(1, 4)
     ring_end(1)
-    gain_send(1, w_two[0, 0:1, :])
     grad_end(1)
     adam(1)
 
@@ -542,52 +564,32 @@
     for i in range(2):
         gain_out[pl.ds(i, LT, stride=2), :] = gsib_s[i] + gsib_r[i]
 
-    def drain(j, c):
-        q_copy(j).wait_send()
-        o_copy(peer(j)).wait_send()
-        s_copy(0, j).wait_send()
-        s_copy(1, j).wait_send()
-        return c
-
-    lax.fori_loop(1, MP, drain, 0)
-
-    @pl.when(sends_cot)
-    def _():
-        def c_drain(j, c):
-            c_copy(j).wait_send()
-            return c
-
-        lax.fori_loop(1, MP, c_drain, 0)
-
+    s_all(1).wait_send()
     for ph in range(2):
         red_copy(ph).wait_send()
     top_copy.wait_send()
     for i in range(2):
-        for q in range(NQ):
-            for way in range(2):
-                for s in range(1, length(way, q) + 1):
-                    ring_copy(i, way, q, s).wait_send()
-            if NY == 2:
-                y_copy(i, q).wait_send()
-
-        def g_drain(j, c):
-            g_copy(i, j).wait_send()
-            return c
-
-        lax.fori_loop(1, DP, g_drain, 0)
+        ring_sent(i)
+        if NY == 2:
+            y_sent(i)
+        g_all(i).wait_send()
     if NY == 2:
         w_copy().wait_send()
     g_pair.wait_send()
 
 
 def hand_on(*refs):
-    n = len(refs) // 2
+    n = len(refs) // 3
     sems = refs[-1]
-    copies = [pltpu.make_async_copy(refs[i], refs[n + i], sems.at[i]) for i in range(n)]
-    for copy in copies:
+    ins = [pltpu.make_async_copy(refs[i], refs[2 * n + i], sems.at[0, i]) for i in range(n)]
+    outs = [pltpu.make_async_copy(refs[2 * n + i], refs[n + i], sems.at[1, i]) for i in range(n)]
+    for copy in ins:
         copy.start()
-    for copy in copies:
-        copy.wait()
+    for into, out in zip(ins, outs):
+        into.wait()
+        out.start()
+    for out in outs:
+        out.wait()
 
 
 def shards(
@@ -605,11 +607,12 @@
     T = rows * slots
     TH = T // 2
     LT = F // HD
-    RB = NY * SH
     H = NZ // 2
+    MX = 4 if MP == 16 else 2
+    YH = MP // MX // 2
     cols = key_cotangent.shape[2]
     DP = NZ * NY
-    FQ = F // NQ
+    FH = F // 2
 
     def tokens(x):
         return native(x).reshape(MP, 2, 2 * LT * slots, HD)
@@ -621,7 +624,7 @@
     B = 2 * LT * slots
     shape = jax.ShapeDtypeStruct
     outs = pl.pallas_call(
-        functools.partial(kernel, (NZ, NY, MP, KVH, F, D, HC, SH)),
+        functools.partial(kernel, (NZ, NY, MP, MX, KVH, F, D, HC, SH)),
         out_shape=(
             shape((SH * 2 * LT, HD), F32),
             shape((SH * 2 * LT, HD), F32),
@@ -640,7 +643,7 @@
             pltpu.VMEM((MP, 2, B, HD), BF16),
             pltpu.VMEM((2, MP, B, HD), BF16),
             pltpu.VMEM((cols, T), BF16),
-            pltpu.VMEM((MP // 2, cols, T), BF16),
+            pltpu.VMEM((MX, YH, cols, T), BF16),
             pltpu.VMEM((SH * 2 * LT, HD), F32),
             pltpu.VMEM((SH * 2 * LT, HD), F32),
             pltpu.VMEM((SH * 2 * LT, HD), F32),
@@ -651,11 +654,11 @@
             pltpu.VMEM((2, 2, SUB, TH), F32),
             pltpu.VMEM((4, T, F), BF16),
             pltpu.VMEM((4, HC, T), BF16),
-            pltpu.VMEM((2, NQ, HC, FQ), BF16),
-            pltpu.VMEM((2, 2, NQ, max(H - 1, 1), RB, FQ), BF16),
-            pltpu.VMEM((2, 2, NQ, H, RB, FQ), BF16),
-            pltpu.VMEM((2, NQ, SH, FQ), BF16),
-            pltpu.VMEM((2, NQ, SH, FQ), BF16),
+            pltpu.VMEM((2, NY, 2, NZ, SH, FH), BF16),
+            pltpu.VMEM((2, 2, NQ, max(H - 1, 1), SH, FH), BF16),
+            pltpu.VMEM((2, 2, NQ, H, SH, FH), BF16),
+            pltpu.VMEM((2, 2, SH, FH), BF16),
+            pltpu.VMEM((2, 2, SH, FH), BF16),
             pltpu.VMEM((2, SH, F), F32),
             pltpu.VMEM((2, SH, F), F32),
             pltpu.VMEM((SH, F), BF16),
@@ -665,16 +668,16 @@
             pltpu.VMEM((2, LT, HD), F32),
             pltpu.VMEM((2, LT, HD), F32),
             dma((9,)),
-            dma((MP,)), dma((MP,)),
-            dma((MP,)), dma((MP // 2,)),
-            dma((MP,)), dma((MP,)),
-            dma((2, MP)), dma((2, MP)),
+            dma, dma((MP // MX,)),
+            dma, dma((YH,)), dma, dma,
+            dma, dma((MP // MX,)),
+            dma((2,)), dma((2,)),
             dma((2,)), dma((2,)),
             dma, dma,
-            dma((2, 2, NQ, H)), dma((2, 2, NQ, H)),
-            dma((2, NQ)), dma((2, NQ)),
+            dma((2, 2)), dma((2, 2, NQ, H)),
+            dma((2,)), dma((2, 2)),
             dma, dma,
-            dma((2, DP)), dma((2, DP)),
+            dma((2,)), dma((2,)),
             dma, dma,
         ],
         compiler_params=pltpu.CompilerParams(
@@ -695,7 +698,7 @@
         out_shape=[shape(x.shape, x.dtype) for x in outs],
         in_specs=[hbm] * 4,
         out_specs=[hbm] * 4,
-        scratch_shapes=[dma((4,))],
+        scratch_shapes=[pltpu.VMEM(x.shape, x.dtype) for x in outs] + [dma((2, 4))],
         compiler_params=pltpu.CompilerParams(vmem_limit_bytes=VMEM_BYTES),
         name="hand_on",
     )(*outs)

time: 109 us -> 76.9 us (0.71)
  Pallas kernels: 108 us -> 76 us
    pallas_call x1, Pallas kernels: 25.2 us -> 1.9 us  [shards(): pl.pallas_call(hand_on, out_shape=[shape(x.shape, x.dtype) for x in outs]...]
    pallas_call x1, Pallas kernels: 82.5 us -> 74.1 us  [shards(): pl.pallas_call(functools.partial(kernel, (NZ, NY, MP, MX, KVH, F, D, HC,...]
where the time goes in v3:
time: 76.9 us; the launch traced here: 76.7 us
  Pallas kernels  76 us (99%)
    pallas_call x1, Pallas kernels, shards(): pl.pallas_call(functools.partial(kernel, (NZ, NY, MP, MX, KVH, F, D, HC,...  74.1 us
    pallas_call x1, Pallas kernels, shards(): pl.pallas_call(hand_on, out_shape=[shape(x.shape, x.dtype) for x in outs]...  1.9 us

profile of v3, /device:TPU:1, one launch (start us, length us, event | category | flops | bytes accessed | tf_op | source)
XLA Modules:
  0.0 76.7 jit_solution(8232340255153005681)
XLA Ops:
  0.6 74.1 %draft_step.1 = (f32[512,128]{1,0:T(8,128)}, f32[512,128]{1,0:T(8,128)}, f32[512,128]{1,0:T(8,128)}, f32[16,128]{1,0:T(8,128)}) custom-call(bf16[16,2,64,128]{3,2,1,0:T(8,128)(2,1)} %bitcast.71, bf16[4,64,1024]{2,1,0:T(8,128)(2,1)} %ck_hbm.1, bf16[4,64,1024]{2,1,0:T(8,128)(2,1)} %cv_hbm.1, bf16[128,128]{1,0:T(8,128)(2,1)} %bitcast.78, ...), custom_call_target="tpu_custom_call" | custom-call | flops 1073741824 | bytes 6291456 | tf_op jit(solution)/shard_map/draft_step/pallas_call | solution.py:626
  74.8 1.9 %hand_on.1 = (f32[512,128]{1,0:T(8,128)}, f32[512,128]{1,0:T(8,128)}, f32[512,128]{1,0:T(8,128)}, f32[16,128]{1,0:T(8,128)}) custom-call(f32[512,128]{1,0:T(8,128)} %get-tuple-element.12.refs_0_, f32[512,128]{1,0:T(8,128)} %get-tuple-element.13.refs_1_, f32[512,128]{1,0:T(8,128)} %get-tuple-element.14.refs_2_, f32[16,128]{1,0:T(8,128)} %get-tuple-element.15.refs_3_), custom_call_target="tpu_custom_call" | custom-call | tf_op jit(solution)/shard_map/hand_on/pallas_call | solution.py:696

commit v4 on v3

--- a/solution.py
+++ b/solution.py
@@ -44,10 +44,10 @@
 
 def kernel(
     dims,
-    q_hbm, ck_hbm, cv_hbm, sk_ref, sv_ref, len_ref, em_hbm, lo_hbm, mi_hbm, cot_ref, acc_ref,
-    jg_ref, ng_ref, ngn_ref, w_hbm, m1_hbm, m2_hbm,
+    q_hbm, ck_hbm, cv_hbm, sk_hbm, sv_hbm, len_ref, em_hbm, lo_hbm, mi_hbm, cot_hbm, acc_hbm,
+    jg_hbm, ng_hbm, ngn_hbm, w_hbm, m1_hbm, m2_hbm,
     w_out, m1_out, m2_out, gain_out,
-    rxq, kbuf, vbuf, outb, emb, lob, mib, topb, csend, cbuf, wbuf, m1buf, m2buf,
+    sk_ref, sv_ref, cot_ref, acc_ref, jg_ref, ng_ref, ngn_ref, rxq, kbuf, vbuf, outb, emb, lob, mib, topb, csend, cbuf, wbuf, m1buf, m2buf,
     gpat, zbuf, ssend, srecv, red, vx, ax, tb, sring, rring, sy, ry, own_t,
     w_two, wsend, wpart, gsend, grecv, gsib_s, gsib_r,
     lsem, q_s, q_r, c_s, c_r, c2_s, c2_r, o_s, o_r, s_s, s_r, red_s, red_r, top_s, top_r,
@@ -97,28 +97,36 @@
         return flipped(d, d_bits, j)
 
     loads = {
+        "cot": pltpu.make_async_copy(cot_hbm, cot_ref, lsem.at[9]),
+        "acc": pltpu.make_async_copy(acc_hbm, acc_ref, lsem.at[10]),
+        "jg": pltpu.make_async_copy(jg_hbm, jg_ref, lsem.at[11]),
         "lo": pltpu.make_async_copy(lo_hbm, lob, lsem.at[0]),
         "mi": pltpu.make_async_copy(mi_hbm, mib, lsem.at[1]),
         "em": pltpu.make_async_copy(em_hbm, emb, lsem.at[2]),
         "q": pltpu.make_async_copy(q_hbm.at[m, g], rxq.at[m], lsem.at[3]),
         "k": pltpu.make_async_copy(ck_hbm.at[pl.ds(2 * g, 2)], kbuf, lsem.at[4]),
         "v": pltpu.make_async_copy(cv_hbm.at[pl.ds(2 * g, 2)], vbuf, lsem.at[5]),
+        "sk": pltpu.make_async_copy(sk_hbm, sk_ref, lsem.at[12]),
+        "sv": pltpu.make_async_copy(sv_hbm, sv_ref, lsem.at[13]),
+        "ng": pltpu.make_async_copy(ng_hbm, ng_ref, lsem.at[14]),
+        "ngn": pltpu.make_async_copy(ngn_hbm, ngn_ref, lsem.at[15]),
         "w": pltpu.make_async_copy(w_hbm, wbuf, lsem.at[6]),
         "m1": pltpu.make_async_copy(m1_hbm, m1buf, lsem.at[7]),
         "m2": pltpu.make_async_copy(m2_hbm, m2buf, lsem.at[8]),
     }
+    bar = pltpu.get_barrier_semaphore()
+
+    greeted = [at(mm=peer(j)) for j in range(MP - 1, 0, -1)]
+    greeted += [at(dd=z * NY + 1 - y)] if NY == 2 else []
+    greeted += [at(dd=zdev(z + 1))] + ([at(dd=zdev(z - 1))] if NZ > 2 else []) + [at(gg=1 - g)]
+    for dev in greeted:
+        pl.semaphore_signal(bar, inc=1, device_id=dev, device_id_type=MESH)
     for load in loads.values():
         load.start()
 
-    bar = pltpu.get_barrier_semaphore()
-
-    for j in range(DP - 1, 0, -1):
-        pl.semaphore_signal(bar, inc=1, device_id=at(dd=dpeer(j)), device_id_type=MESH)
-    for j in range(MP - 1, 0, -1):
-        pl.semaphore_signal(bar, inc=1, device_id=at(mm=peer(j)), device_id_type=MESH)
-    pl.semaphore_signal(bar, inc=1, device_id=at(gg=1 - g), device_id_type=MESH)
-
     RD = 4 * MP
+    loads["cot"].wait()
+    loads["acc"].wait()
     ct = cot_ref[...].astype(F32).reshape(RD // 2, 2, 4, cot_ref.shape[2])
     ct = jnp.concatenate([ct[:, 0], ct[:, 1]], axis=1).reshape(MP, 2, SUB, cot_ref.shape[2])
     ct = jnp.concatenate([ct[:, 0], ct[:, 1]], axis=0).reshape(T, cot_ref.shape[2])
@@ -136,6 +144,7 @@
     csend[...] = (ct.T * weight).astype(BF16)
 
     sub8 = lax.broadcasted_iota(jnp.int32, (1, SUB, HD), 1) < 4
+    loads["jg"].wait()
     for a in range(3):
         for lp in range(LT // 2):
             lower = jg_ref[a : a + 1, 2 * lp * HD : (2 * lp + 1) * HD]
@@ -200,7 +209,7 @@
         w_two[i] = w.reshape(SH, LT, HD).reshape(SH, F)
     wsend[...] = w_two[1].astype(BF16)
 
-    pl.semaphore_wait(bar, DP - 1 + MP - 1 + 1)
+    pl.semaphore_wait(bar, len(greeted))
 
     def q_copy(j):
         dst = peer(j)
@@ -271,6 +280,8 @@
     loads["k"].wait()
     loads["v"].wait()
     loads["q"].wait()
+    for key in ("sk", "sv", "ng", "ngn"):
+        loads[key].wait()
     CP = 64
     SR = KVH * 4
     QR = 32
@@ -331,31 +342,30 @@
     def inv(total):
         return lax.rsqrt(total * (1.0 / D) + EPS)
 
+    CW = HC // (YH * MX)
+
     def scale_cot(n, row):
         for b in range(YH):
             for x in range(MX):
-                rows = slice((b * MX + x) * CW, (b * MX + x + 1) * CW)
-                ax[n, rows, :] = (cbuf[x, b].astype(F32) * row).astype(BF16)
-
-    CW = HC // (YH * MX)
+                scaled = (cbuf[x, b].astype(F32) * row).astype(BF16)
+                for yy in range(NY):
+                    ax[n, yy, b * MX + x] = scaled[yy * SH : (yy + 1) * SH]
+
     scale = (2.0 * D) ** -0.5
-    CB = min(HC, 256)
-    ZB = CB // (NY * SH)
-
-    def tile(i, q, terms):
-        cols = slice(q * FH // 2, (q + 1) * FH // 2)
-        here = slice((q % 2) * FH // 2, (q % 2 + 1) * FH // 2)
-        for n in range(HC // CB):
+
+    def tile(i, yy, ch, terms):
+        for h in range(2):
+            cols = slice(ch * FH + h * FH // 2, ch * FH + (h + 1) * FH // 2)
             total = None
             for n_x, gain in terms:
-                part = jnp.dot(ax[n_x, n * CB : (n + 1) * CB, :], vx[n_x, :, cols], preferred_element_type=F32)
+                part = jnp.dot(
+                    ax[n_x, yy].reshape(NZ * SH, T), vx[n_x, :, cols], preferred_element_type=F32
+                )
                 if gain is not None:
                     part = part * jg_ref[gain : gain + 1, cols]
                 total = part if total is None else total + part
             total = (total * (ng_ref[i : i + 1, cols] * scale)).astype(BF16)
-            total = total.reshape(ZB, NY, SH, FH // 2)
-            for yy in range(NY):
-                tb[i, yy, q // 2, n * ZB : (n + 1) * ZB, :, here] = total[:, yy]
+            tb[i, yy, ch, :, :, h * FH // 2 : (h + 1) * FH // 2] = total.reshape(NZ, SH, FH // 2)
 
     CHUNKS = [q for q in range(NQ) if NY == 2 or q >= 2]
 
@@ -400,12 +410,9 @@
         remote(some, some, ring_s.at[i, 1], ring_r.at[i, 0, 0, 0], at(dd=zdev(z + 1))).wait_send()
 
     def gradient(i, terms):
-        for ch in range(2):
-            tile(i, 2 * ch, terms)
-            tile(i, 2 * ch + 1, terms)
-            for q in CHUNKS:
-                if q % 2 == ch:
-                    ring_step(i, 1, q)
+        for q in CHUNKS:
+            tile(i, y_of(q), q % 2, terms)
+            ring_step(i, 1, q)
 
     def y_copy(i, ch):
         return remote(sy.at[i, ch], ry.at[i, ch], y_s.at[i], y_r.at[i, ch], at(dd=z * NY + 1 - y))
@@ -496,15 +503,11 @@
     s_begin(1)
     top_copy = remote(topb.at[g], topb.at[g], top_s, top_r, at(gg=1 - g))
     top_copy.start()
-    if NY == 2:
-        w_copy().start()
     relayout_all(3, lambda i, gg: topb[gg, i], g)
     if H >= 2:
         ring_steps(0, 2)
     remote(topb.at[g], topb.at[1 - g], top_s, top_r, at(gg=1 - g)).wait_recv()
     relayout_all(3, lambda i, gg: topb[gg, i], 1 - g)
-    if H >= 3:
-        ring_steps(0, 3)
 
     def sent(block, count, sem, r):
         some = block.at[0:count]
@@ -517,10 +520,12 @@
 
     @pl.when(sends_cot)
     def _():
-        some = ax.at[0, 0 : (MY - 1) * CW]
+        some = ax.at[0, 0, 0 : (MY - 1) * CW // SH]
         remote(some, some, c_s, c_r.at[0], at(mm=peer(1))).wait_send()
 
     s_reduce(1)
+    if H >= 3:
+        ring_steps(0, 3)
     remote(red.at[1, g], red.at[1, 1 - g], red_s.at[1], red_r.at[1], at(gg=1 - g)).wait_recv()
 
     rl, rv, rt = inv(sums(0, 1)), inv(sums(0, 2)), inv(sums(1, 0))
@@ -536,6 +541,8 @@
     scale_cot(3, rt * rj)
     gradient(1, ((1, 0), (2, 1), (3, 2)))
 
+    if NY == 2:
+        w_copy().start()
     if H >= 4:
         ring_steps(0, 4)
     if H >= 2:
@@ -543,6 +550,8 @@
     ring_end(0)
     if H >= 3:
         ring_steps(1, 3)
+    if H >= 4:
+        ring_steps(1, 4)
     loads["m1"].wait()
     loads["m2"].wait()
     grad_end(0)
@@ -550,8 +559,6 @@
     adam(0)
     if NY == 2:
         w_copy().wait_recv()
-    if H >= 4:
-        ring_steps(1, 4)
     ring_end(1)
     grad_end(1)
     adam(1)
@@ -579,17 +586,13 @@
 
 
 def hand_on(*refs):
-    n = len(refs) // 3
+    n = len(refs) // 2
     sems = refs[-1]
-    ins = [pltpu.make_async_copy(refs[i], refs[2 * n + i], sems.at[0, i]) for i in range(n)]
-    outs = [pltpu.make_async_copy(refs[2 * n + i], refs[n + i], sems.at[1, i]) for i in range(n)]
-    for copy in ins:
+    copies = [pltpu.make_async_copy(refs[i], refs[n + i], sems.at[i]) for i in range(n)]
+    for copy in copies:
         copy.start()
-    for into, out in zip(ins, outs):
-        into.wait()
-        out.start()
-    for out in outs:
-        out.wait()
+    for copy in copies:
+        copy.wait()
 
 
 def shards(
@@ -626,14 +629,21 @@
     outs = pl.pallas_call(
         functools.partial(kernel, (NZ, NY, MP, MX, KVH, F, D, HC, SH)),
         out_shape=(
-            shape((SH * 2 * LT, HD), F32),
-            shape((SH * 2 * LT, HD), F32),
-            shape((SH * 2 * LT, HD), F32),
-            shape((2 * LT, HD), F32),
+            pltpu.VMEM((SH * 2 * LT, HD), F32),
+            pltpu.VMEM((SH * 2 * LT, HD), F32),
+            pltpu.VMEM((SH * 2 * LT, HD), F32),
+            pltpu.VMEM((2 * LT, HD), F32),
         ),
-        in_specs=[hbm, hbm, hbm, vmem, vmem, smem, hbm, hbm, hbm] + [vmem] * 5 + [hbm, hbm, hbm],
+        in_specs=[hbm] * 5 + [smem] + [hbm] * 11,
         out_specs=(vmem, vmem, vmem, vmem),
         scratch_shapes=[
+            pltpu.VMEM((KVH * 16, HD), BF16),
+            pltpu.VMEM((KVH * 16, HD), BF16),
+            pltpu.VMEM(key_cotangent.shape, BF16),
+            pltpu.VMEM((1, rows), jnp.int32),
+            pltpu.VMEM((3, F), F32),
+            pltpu.VMEM((2, F), F32),
+            pltpu.VMEM((2 * LT, HD), F32),
             pltpu.VMEM((MP, B, HD), BF16),
             pltpu.VMEM((2, 64, KW), BF16),
             pltpu.VMEM((2, 64, KW), BF16),
@@ -653,7 +663,7 @@
             pltpu.VMEM((2, MP, SUB, TH), F32),
             pltpu.VMEM((2, 2, SUB, TH), F32),
             pltpu.VMEM((4, T, F), BF16),
-            pltpu.VMEM((4, HC, T), BF16),
+            pltpu.VMEM((4, NY, NZ, SH, T), BF16),
             pltpu.VMEM((2, NY, 2, NZ, SH, FH), BF16),
             pltpu.VMEM((2, 2, NQ, max(H - 1, 1), SH, FH), BF16),
             pltpu.VMEM((2, 2, NQ, H, SH, FH), BF16),
@@ -667,7 +677,7 @@
             pltpu.VMEM((2, DP, LT, HD), F32),
             pltpu.VMEM((2, LT, HD), F32),
             pltpu.VMEM((2, LT, HD), F32),
-            dma((9,)),
+            dma((16,)),
             dma, dma((MP // MX,)),
             dma, dma((YH,)), dma, dma,
             dma, dma((MP // MX,)),
@@ -696,10 +706,10 @@
     outs = pl.pallas_call(
         hand_on,
         out_shape=[shape(x.shape, x.dtype) for x in outs],
-        in_specs=[hbm] * 4,
+        in_specs=[vmem] * 4,
         out_specs=[hbm] * 4,
-        scratch_shapes=[pltpu.VMEM(x.shape, x.dtype) for x in outs] + [dma((2, 4))],
-        compiler_params=pltpu.CompilerParams(vmem_limit_bytes=VMEM_BYTES),
+        scratch_shapes=[dma((4,))],
+        compiler_params=pltpu.CompilerParams(vmem_limit_bytes=VMEM_BYTES // 8),
         name="hand_on",
     )(*outs)
     new = [from_native(x, SH, 2, F) for x in outs[:3]]

time: 76.9 us -> 70.1 us (0.912)
  Pallas kernels: 76 us -> 69.3 us
    pallas_call x1, Pallas kernels: 74.1 us -> 68.4 us  [shards(): pl.pallas_call(functools.partial(kernel, (NZ, NY, MP, MX, KVH, F, D, HC,...]
    pallas_call x1, Pallas kernels: 1.9 us -> 0.91 us  [shards(): pl.pallas_call(hand_on, out_shape=[shape(x.shape, x.dtype) for x in outs]...]
where the time goes in v4:
time: 70.1 us; the launch traced here: 69.9 us
  Pallas kernels  69.3 us (99%)
    pallas_call x1, Pallas kernels, shards(): pl.pallas_call(functools.partial(kernel, (NZ, NY, MP, MX, KVH, F, D, HC,...  68.4 us

profile of v4, /device:TPU:1, one launch (start us, length us, event | category | flops | bytes accessed | tf_op | source)
XLA Modules:
  0.0 69.9 jit_solution(6028934691912252877)
XLA Ops:
  0.6 68.4 %draft_step.1 = (f32[512,128]{1,0:T(8,128)S(1)}, f32[512,128]{1,0:T(8,128)S(1)}, f32[512,128]{1,0:T(8,128)S(1)}, f32[16,128]{1,0:T(8,128)S(1)}) custom-call(bf16[16,2,64,128]{3,2,1,0:T(8,128)(2,1)} %bitcast.71, bf16[4,64,1024]{2,1,0:T(8,128)(2,1)} %ck_hbm.1, bf16[4,64,1024]{2,1,0:T(8,128)(2,1)} %cv_hbm.1, bf16[128,128]{1,0:T(8,128)(2,1)} %bitcast.78, ...), custom_call_target="tpu_custom_call" | custom-call | flops 1073741824 | bytes 6291456 | tf_op jit(solution)/shard_map/draft_step/pallas_call | solution.py:629
  69.0 0.9 %hand_on.1 = (f32[512,128]{1,0:T(8,128)}, f32[512,128]{1,0:T(8,128)}, f32[512,128]{1,0:T(8,128)}, f32[16,128]{1,0:T(8,128)}) custom-call(f32[512,128]{1,0:T(8,128)S(1)} %get-tuple-element.12.refs_0_, f32[512,128]{1,0:T(8,128)S(1)} %get-tuple-element.13.refs_1_, f32[512,128]{1,0:T(8,128)S(1)} %get-tuple-element.14.refs_2_, ...), custom_call_target="tpu_custom_call" | custom-call | tf_op jit(solution)/shard_map/hand_on/pallas_call | solution.py:706

commit v5 on v4

--- a/solution.py
+++ b/solution.py
@@ -48,10 +48,10 @@
     jg_hbm, ng_hbm, ngn_hbm, w_hbm, m1_hbm, m2_hbm,
     w_out, m1_out, m2_out, gain_out,
     sk_ref, sv_ref, cot_ref, acc_ref, jg_ref, ng_ref, ngn_ref, rxq, kbuf, vbuf, outb, emb, lob, mib, topb, csend, cbuf, wbuf, m1buf, m2buf,
-    gpat, zbuf, ssend, srecv, red, vx, ax, tb, sring, rring, sy, ry, own_t,
-    w_two, wsend, wpart, gsend, grecv, gsib_s, gsib_r,
+    gpat, zbuf, ssend, srecv, srecv2, red, vx, ax, tb, sring, rring, sy, ry, own_t,
+    w_two, wz, gsend, grecv, gsib_s, gsib_r,
     lsem, q_s, q_r, c_s, c_r, c2_s, c2_r, o_s, o_r, s_s, s_r, red_s, red_r, top_s, top_r,
-    ring_s, ring_r, y_s, y_r, wx_s, wx_r, g_s, g_r, gx_s, gx_r,
+    ring_s, ring_r, y_s, y_r, wx_s, wx_r, wz_s, wz_r, g_s, g_r, gx_s, gx_r,
 ):
     NZ, NY, MP, MX, KVH, F, D, HC, SH = dims
     MY = MP // MX
@@ -206,8 +206,11 @@
     loads["w"].wait()
     for i in range(2):
         w = wbuf[pl.ds(i, SH * LT, stride=2), :].astype(BF16).astype(F32)
-        w_two[i] = w.reshape(SH, LT, HD).reshape(SH, F)
-    wsend[...] = w_two[1].astype(BF16)
+        w = w.reshape(SH, LT, HD).reshape(SH, F)
+        if i == 0:
+            w_two[...] = w
+        else:
+            wz[0, 1] = w.astype(BF16)
 
     pl.semaphore_wait(bar, len(greeted))
 
@@ -248,30 +251,25 @@
     def c_end():
         remote(cbuf.at[0 : MX - 1], cbuf.at[0 : MX - 1], c2_s, c2_r, at(mm=peer(1))).wait_recv()
 
-    def s_copy(ph, j):
-        return remote(ssend.at[ph], srecv.at[ph, m], s_s.at[ph], s_r.at[ph], at(mm=peer(j)))
-
-    def s_begin(ph):
-        for j in range(MP - 1, 0, -1):
-            s_copy(ph, j).start()
-        srecv[ph, m] = ssend[ph]
-
-    s_begin(0)
-
-    def s_all(ph):
-        some = srecv.at[ph, 0 : MP - 1]
-        return remote(some, some, s_s.at[ph], s_r.at[ph], at(mm=peer(1)))
-
-    def red_copy(ph):
-        return remote(red.at[ph, g], red.at[ph, g], red_s.at[ph], red_r.at[ph], at(gg=1 - g))
-
-    def s_reduce(ph):
-        s_all(ph).wait_recv()
-        red[ph, g] = jnp.sum(srecv[ph], axis=0)
-        red_copy(ph).start()
+    for j in range(MP - 1, 0, -1):
+        remote(ssend.at[0], srecv.at[m], s_s.at[0], s_r.at[0], at(mm=peer(j))).start()
+    srecv[m] = ssend[0]
+
+    def s_all():
+        some = srecv.at[0 : MP - 1]
+        return remote(some, some, s_s.at[0], s_r.at[0], at(mm=peer(1)))
+
+    def red_copy():
+        return remote(red.at[0, g], red.at[0, g], red_s, red_r, at(gg=1 - g))
 
     def w_copy():
-        return remote(wsend, wpart, wx_s, wx_r, at(dd=z * NY + 1 - y))
+        return remote(wz.at[0, 1], wz.at[0, 0], wx_s, wx_r, at(dd=z * NY + 1 - y))
+
+    def wz_copy(way, yo):
+        return remote(wz.at[0, yo], wz.at[1 + way, yo], wz_s, wz_r.at[way, yo], at(dd=zdev(z + 1 - 2 * way)))
+
+    for way in range(2):
+        wz_copy(way, 1).start()
 
     for gg in range(2):
         relayout_all(1, lambda i, gg: lob[i, gg], gg)
@@ -308,8 +306,8 @@
             s = dot_nt(qk, keys) * (HD**-0.5)
             s = jnp.where(live, s, -1e30)
             top = jnp.max(s, axis=-1, keepdims=True)
-            e = jnp.where(live, jnp.exp(s - top), 0.0)
-            p = (e / jnp.sum(e, axis=-1, keepdims=True)).astype(BF16)
+            e = jnp.exp(s - top)
+            p = (e * (1.0 / jnp.sum(e, axis=-1, keepdims=True))).astype(BF16)
             o = jnp.dot(p, vals, preferred_element_type=F32).astype(BF16)
             yield 2 * k, qrows, o[:QR]
             yield 2 * k + 1, qrows, o[QR:]
@@ -319,6 +317,8 @@
         count = MX - 1 if jy == 0 else MX
         some = rxq.at[0:count]
         remote(some, some, q_s, q_r.at[yl], at(mm=peer(1))).wait_recv()
+        if jy == 1 and NY == 2:
+            w_copy().start()
         done = []
         for h in range(MX // 2):
             done += list(attend(yl * (MX // 2) + h))
@@ -331,10 +331,12 @@
             c_turn()
     topb[g, m] = outb[m]
 
-    s_reduce(0)
+    s_all().wait_recv()
+    red[0, g] = jnp.sum(srecv[...], axis=0)
+    red_copy().start()
 
     c_end()
-    remote(red.at[0, g], red.at[0, 1 - g], red_s.at[0], red_r.at[0], at(gg=1 - g)).wait_recv()
+    remote(red.at[0, g], red.at[0, 1 - g], red_s, red_r, at(gg=1 - g)).wait_recv()
 
     def sums(ph, n):
         return jnp.concatenate([red[ph, 0, n : n + 1, :], red[ph, 1, n : n + 1, :]], axis=1)
@@ -386,16 +388,30 @@
             at(dd=zdev(z + step)),
         )
 
+    gain_terms = [[], []]
+
+    def gain_term(q, t, place):
+        ch = q % 2
+        part = t * wz[place, q // 2, :, ch * FH : (ch + 1) * FH].astype(F32)
+        gain_terms[ch].append(jnp.sum(part.reshape(SH // SUB, SUB, FH), axis=0))
+
     def ring_step(i, s, q):
         for way in range(2):
-            if s > length(way, q):
+            n = length(way, q)
+            if s > n:
                 continue
             if s > 1:
                 ring_copy(i, way, q, s - 1).wait_recv()
                 step = 1 if way == 0 else -1
-                own = term(i, q, z + step * (length(way, q) + 1 - s))[...].astype(F32)
-                sring[i, way, q, s - 2] = (own + rring[i, way, q, s - 2].astype(F32)).astype(BF16)
+                own = term(i, q, z + step * (n + 1 - s))[...].astype(F32)
+                t = own + rring[i, way, q, s - 2].astype(F32)
+                sring[i, way, q, s - 2] = t.astype(BF16)
             ring_copy(i, way, q, s).start()
+            if i == 1 and s == n:
+                if s == 1:
+                    step = 1 if way == 0 else -1
+                    t = term(i, q, z + step)[...].astype(F32)
+                gain_term(q, t, 2 - way)
 
     def ring_steps(i, s):
         for q in CHUNKS:
@@ -421,10 +437,8 @@
         remote(sy.at[i], ry.at[i], y_s.at[i], y_r.at[i, 0], at(dd=z * NY + 1 - y)).wait_send()
 
     def ring_end(i):
-        gain = [None, None]
         for q in CHUNKS:
             ch = q % 2
-            cols = slice(ch * FH, (ch + 1) * FH)
             t = term(i, q, z)[...].astype(F32)
             for way in range(2):
                 n = length(way, q)
@@ -434,15 +448,8 @@
             if q < 2:
                 sy[i, ch] = t.astype(BF16)
                 y_copy(i, ch).start()
-                if i == 1:
-                    gain[ch] = t * wpart[:, cols].astype(F32)
             else:
-                own_t[i, :, cols] = t
-                if i == 1:
-                    part = t * w_two[1, :, cols]
-                    gain[ch] = part if gain[ch] is None else gain[ch] + part
-        if i == 1:
-            gain_send(1, jnp.sum(jnp.concatenate(gain, axis=1), axis=0, keepdims=True))
+                own_t[i, :, ch * FH : (ch + 1) * FH] = t
 
     def grad_end(i):
         if NY == 2:
@@ -451,23 +458,26 @@
                 y_copy(i, ch).wait_recv()
                 own_t[i, :, cols] = own_t[i, :, cols] + ry[i, ch].astype(F32)
 
-    def g_copy(i, j):
-        return remote(gsend.at[i], grecv.at[i, d], g_s.at[i], g_r.at[i], at(dd=dpeer(j)))
-
-    def gain_send(i, row):
-        tiles = jnp.concatenate([row[:, t * HD : (t + 1) * HD] for t in range(LT)], axis=0)
-        gsend[i] = tiles / ngn_ref[pl.ds(i, LT, stride=2), :]
+    def g_copy(j):
+        return remote(gsend, grecv.at[d], g_s, g_r, at(dd=dpeer(j)))
+
+    def gain_send():
+        ones = [jnp.sum(own_t[0] * w_two[...], axis=0, keepdims=True)]
+        ones.append(
+            jnp.concatenate([jnp.sum(sum(parts), axis=0, keepdims=True) for parts in gain_terms], axis=1)
+        )
+        tiles = []
+        for i in range(2):
+            row = jnp.concatenate([ones[i][:, t * HD : (t + 1) * HD] for t in range(LT)], axis=0)
+            tiles.append(row / ngn_ref[pl.ds(i, LT, stride=2), :])
+        gsend[...] = jnp.concatenate(tiles, axis=0).astype(BF16)
         for j in range(DP - 1, 0, -1):
-            g_copy(i, j).start()
-        grecv[i, d] = gsend[i]
-
-    def g_all(i):
-        some = grecv.at[i, 0 : DP - 1]
-        return remote(some, some, g_s.at[i], g_r.at[i], at(dd=dpeer(1)))
-
-    def gain_total(i):
-        g_all(i).wait_recv()
-        return jnp.sum(grecv[i], axis=0)
+            g_copy(j).start()
+        grecv[d] = gsend[...]
+
+    def g_all():
+        some = grecv.at[0 : DP - 1]
+        return remote(some, some, g_s, g_r, at(dd=dpeer(1)))
 
     def adam(i):
         rows = pl.ds(i, SH * LT, stride=2)
@@ -500,12 +510,27 @@
 
         lax.fori_loop(0, MX, stats1, 0, unroll=2)
     ssend[1] = row_sums(4)
-    s_begin(1)
+    def s2_copy(gg, j):
+        return remote(ssend.at[1], srecv2.at[g * MP + m], s_s.at[1], s_r.at[1], at(gg=gg, mm=peer(j)))
+
+    def s2_all():
+        some = srecv2.at[0 : 2 * MP - 1]
+        return remote(some, some, s_s.at[1], s_r.at[1], at(mm=peer(1)))
+
+    for j in range(MP - 1, -1, -1):
+        if j:
+            s2_copy(g, j).start()
+        s2_copy(1 - g, j).start()
+    srecv2[g * MP + m] = ssend[1]
     top_copy = remote(topb.at[g], topb.at[g], top_s, top_r, at(gg=1 - g))
     top_copy.start()
     relayout_all(3, lambda i, gg: topb[gg, i], g)
     if H >= 2:
         ring_steps(0, 2)
+    if NY == 2:
+        w_copy().wait_recv()
+        for way in range(2):
+            wz_copy(way, 0).start()
     remote(topb.at[g], topb.at[1 - g], top_s, top_r, at(gg=1 - g)).wait_recv()
     relayout_all(3, lambda i, gg: topb[gg, i], 1 - g)
 
@@ -513,9 +538,11 @@
         some = block.at[0:count]
         remote(some, some, sem, r, at(mm=peer(1))).wait_send()
 
+    if H >= 3:
+        ring_steps(0, 3)
     sent(rxq, MP - 1, q_s, q_r.at[0])
     sent(outb, MP - 1, o_s, o_r.at[0])
-    s_all(0).wait_send()
+    s_all().wait_send()
     sent(cbuf, MX - 1, c2_s, c2_r)
 
     @pl.when(sends_cot)
@@ -523,10 +550,9 @@
         some = ax.at[0, 0, 0 : (MY - 1) * CW // SH]
         remote(some, some, c_s, c_r.at[0], at(mm=peer(1))).wait_send()
 
-    s_reduce(1)
-    if H >= 3:
-        ring_steps(0, 3)
-    remote(red.at[1, g], red.at[1, 1 - g], red_s.at[1], red_r.at[1], at(gg=1 - g)).wait_recv()
+    s2_all().wait_recv()
+    for gg in range(2):
+        red[1, gg] = jnp.sum(srecv2[gg * MP : (gg + 1) * MP], axis=0)
 
     rl, rv, rt = inv(sums(0, 1)), inv(sums(0, 2)), inv(sums(1, 0))
     joined = (
@@ -539,10 +565,11 @@
     scale_cot(1, rl * rj)
     scale_cot(2, rv * rj)
     scale_cot(3, rt * rj)
+    for way in range(2):
+        for yo in range(2 - NY, 2):
+            wz_copy(way, yo).wait_recv()
     gradient(1, ((1, 0), (2, 1), (3, 2)))
 
-    if NY == 2:
-        w_copy().start()
     if H >= 4:
         ring_steps(0, 4)
     if H >= 2:
@@ -550,38 +577,41 @@
     ring_end(0)
     if H >= 3:
         ring_steps(1, 3)
+    for q in CHUNKS:
+        gain_term(q, term(1, q, z)[...].astype(F32), 0)
     if H >= 4:
         ring_steps(1, 4)
     loads["m1"].wait()
     loads["m2"].wait()
     grad_end(0)
-    gain_send(0, jnp.sum(own_t[0] * w_two[0], axis=0, keepdims=True))
+    gain_send()
     adam(0)
-    if NY == 2:
-        w_copy().wait_recv()
     ring_end(1)
     grad_end(1)
     adam(1)
 
-    for i in range(2):
-        gsib_s[i] = gain_total(i)
-    g_pair = remote(gsib_s, gsib_r, gx_s, gx_r, at(gg=1 - g))
-    g_pair.start()
-    g_pair.wait_recv()
-    for i in range(2):
-        gain_out[pl.ds(i, LT, stride=2), :] = gsib_s[i] + gsib_r[i]
-
-    s_all(1).wait_send()
-    for ph in range(2):
-        red_copy(ph).wait_send()
+    s2_all().wait_send()
+    red_copy().wait_send()
     top_copy.wait_send()
     for i in range(2):
         ring_sent(i)
         if NY == 2:
             y_sent(i)
-        g_all(i).wait_send()
     if NY == 2:
         w_copy().wait_send()
+    for way in range(2):
+        for yo in range(2 - NY, 2):
+            wz_copy(way, yo).wait_send()
+
+    g_all().wait_recv()
+    gsib_s[...] = jnp.sum(grecv[...].astype(F32), axis=0)
+    g_pair = remote(gsib_s, gsib_r, gx_s, gx_r, at(gg=1 - g))
+    g_pair.start()
+    g_all().wait_send()
+    g_pair.wait_recv()
+    total = gsib_s[...] + gsib_r[...]
+    for i in range(2):
+        gain_out[pl.ds(i, LT, stride=2), :] = total[i * LT : (i + 1) * LT]
     g_pair.wait_send()
 
 
@@ -660,7 +690,8 @@
             pltpu.VMEM((3, LT // 2, SUB, HD), F32),
             pltpu.VMEM((SUB, TH, HD), F32),
             pltpu.VMEM((2, SUB, TH), F32),
-            pltpu.VMEM((2, MP, SUB, TH), F32),
+            pltpu.VMEM((MP, SUB, TH), F32),
+            pltpu.VMEM((2 * MP, SUB, TH), F32),
             pltpu.VMEM((2, 2, SUB, TH), F32),
             pltpu.VMEM((4, T, F), BF16),
             pltpu.VMEM((4, NY, NZ, SH, T), BF16),
@@ -670,24 +701,24 @@
             pltpu.VMEM((2, 2, SH, FH), BF16),
             pltpu.VMEM((2, 2, SH, FH), BF16),
             pltpu.VMEM((2, SH, F), F32),
-            pltpu.VMEM((2, SH, F), F32),
-            pltpu.VMEM((SH, F), BF16),
-            pltpu.VMEM((SH, F), BF16),
-            pltpu.VMEM((2, LT, HD), F32),
-            pltpu.VMEM((2, DP, LT, HD), F32),
-            pltpu.VMEM((2, LT, HD), F32),
-            pltpu.VMEM((2, LT, HD), F32),
+            pltpu.VMEM((SH, F), F32),
+            pltpu.VMEM((3, 2, SH, F), BF16),
+            pltpu.VMEM((2 * LT, HD), BF16),
+            pltpu.VMEM((DP, 2 * LT, HD), BF16),
+            pltpu.VMEM((2 * LT, HD), F32),
+            pltpu.VMEM((2 * LT, HD), F32),
             dma((16,)),
             dma, dma((MP // MX,)),
             dma, dma((YH,)), dma, dma,
             dma, dma((MP // MX,)),
             dma((2,)), dma((2,)),
-            dma((2,)), dma((2,)),
+            dma, dma,
             dma, dma,
             dma((2, 2)), dma((2, 2, NQ, H)),
             dma((2,)), dma((2, 2)),
             dma, dma,
-            dma((2,)), dma((2,)),
+            dma, dma((2, 2)),
+            dma, dma,
             dma, dma,
         ],
         compiler_params=pltpu.CompilerParams(

time: 70.1 us -> 70.3 us (level)
  no operation moved by 1% of the time
where the time goes in v5:
time: 70.3 us; the launch traced here: 70.1 us
  Pallas kernels  69.5 us (99%)
    pallas_call x1, Pallas kernels, shards(): pl.pallas_call(functools.partial(kernel, (NZ, NY, MP, MX, KVH, F, D, HC,...  68.6 us

profile of v5, /device:TPU:1, one launch (start us, length us, event | category | flops | bytes accessed | tf_op | source)
XLA Modules:
  0.0 70.1 jit_solution(4570706870340686218)
XLA Ops:
  0.6 68.6 %draft_step.1 = (f32[512,128]{1,0:T(8,128)S(1)}, f32[512,128]{1,0:T(8,128)S(1)}, f32[512,128]{1,0:T(8,128)S(1)}, f32[16,128]{1,0:T(8,128)S(1)}) custom-call(bf16[16,2,64,128]{3,2,1,0:T(8,128)(2,1)} %bitcast.71, bf16[4,64,1024]{2,1,0:T(8,128)(2,1)} %ck_hbm.1, bf16[4,64,1024]{2,1,0:T(8,128)(2,1)} %cv_hbm.1, bf16[128,128]{1,0:T(8,128)(2,1)} %bitcast.78, ...), custom_call_target="tpu_custom_call" | custom-call | flops 1073741824 | bytes 6291456 | tf_op jit(solution)/shard_map/draft_step/pallas_call | solution.py:659
  69.2 0.9 %hand_on.1 = (f32[512,128]{1,0:T(8,128)}, f32[512,128]{1,0:T(8,128)}, f32[512,128]{1,0:T(8,128)}, f32[16,128]{1,0:T(8,128)}) custom-call(f32[512,128]{1,0:T(8,128)S(1)} %get-tuple-element.12.refs_0_, f32[512,128]{1,0:T(8,128)S(1)} %get-tuple-element.13.refs_1_, f32[512,128]{1,0:T(8,128)S(1)} %get-tuple-element.14.refs_2_, ...), custom_call_target="tpu_custom_call" | custom-call | tf_op jit(solution)/shard_map/hand_on/pallas_call | solution.py:737

commit v6 on v5

--- a/solution.py
+++ b/solution.py
@@ -210,7 +210,7 @@
         if i == 0:
             w_two[...] = w
         else:
-            wz[0, 1] = w.astype(BF16)
+            wz[1] = w.astype(BF16)
 
     pl.semaphore_wait(bar, len(greeted))
 
@@ -263,13 +263,13 @@
         return remote(red.at[0, g], red.at[0, g], red_s, red_r, at(gg=1 - g))
 
     def w_copy():
-        return remote(wz.at[0, 1], wz.at[0, 0], wx_s, wx_r, at(dd=z * NY + 1 - y))
-
-    def wz_copy(way, yo):
-        return remote(wz.at[0, yo], wz.at[1 + way, yo], wz_s, wz_r.at[way, yo], at(dd=zdev(z + 1 - 2 * way)))
+        return remote(wz.at[1], wz.at[0], wx_s, wx_r, at(dd=z * NY + 1 - y))
+
+    def wz_copy(way):
+        return remote(wz.at[1], wz.at[2 + way], wz_s, wz_r.at[way], at(dd=zdev(z + 1 - 2 * way)))
 
     for way in range(2):
-        wz_copy(way, 1).start()
+        wz_copy(way).start()
 
     for gg in range(2):
         relayout_all(1, lambda i, gg: lob[i, gg], gg)
@@ -317,8 +317,6 @@
         count = MX - 1 if jy == 0 else MX
         some = rxq.at[0:count]
         remote(some, some, q_s, q_r.at[yl], at(mm=peer(1))).wait_recv()
-        if jy == 1 and NY == 2:
-            w_copy().start()
         done = []
         for h in range(MX // 2):
             done += list(attend(yl * (MX // 2) + h))
@@ -346,12 +344,11 @@
 
     CW = HC // (YH * MX)
 
-    def scale_cot(n, row):
+    def scale_cot(n, row, yy):
+        here = pl.ds(pl.multiple_of(yy * SH, SH), SH)
         for b in range(YH):
             for x in range(MX):
-                scaled = (cbuf[x, b].astype(F32) * row).astype(BF16)
-                for yy in range(NY):
-                    ax[n, yy, b * MX + x] = scaled[yy * SH : (yy + 1) * SH]
+                ax[n, yy, b * MX + x] = (cbuf[x, b, here, :].astype(F32) * row).astype(BF16)
 
     scale = (2.0 * D) ** -0.5
 
@@ -392,7 +389,7 @@
 
     def gain_term(q, t, place):
         ch = q % 2
-        part = t * wz[place, q // 2, :, ch * FH : (ch + 1) * FH].astype(F32)
+        part = t * wz[place, :, ch * FH : (ch + 1) * FH].astype(F32)
         gain_terms[ch].append(jnp.sum(part.reshape(SH // SUB, SUB, FH), axis=0))
 
     def ring_step(i, s, q):
@@ -407,11 +404,11 @@
                 t = own + rring[i, way, q, s - 2].astype(F32)
                 sring[i, way, q, s - 2] = t.astype(BF16)
             ring_copy(i, way, q, s).start()
-            if i == 1 and s == n:
+            if i == 1 and s == n and q >= 2:
                 if s == 1:
                     step = 1 if way == 0 else -1
                     t = term(i, q, z + step)[...].astype(F32)
-                gain_term(q, t, 2 - way)
+                gain_term(q, t, 3 - way)
 
     def ring_steps(i, s):
         for q in CHUNKS:
@@ -425,8 +422,11 @@
         some = rring.at[i, :, 0:ways, 0]
         remote(some, some, ring_s.at[i, 1], ring_r.at[i, 0, 0, 0], at(dd=zdev(z + 1))).wait_send()
 
-    def gradient(i, terms):
+    def gradient(i, terms, rows):
         for q in CHUNKS:
+            if q % 2 == 0:
+                for (n, _), row in zip(terms, rows):
+                    scale_cot(n, row, y_of(q))
             tile(i, y_of(q), q % 2, terms)
             ring_step(i, 1, q)
 
@@ -439,6 +439,8 @@
     def ring_end(i):
         for q in CHUNKS:
             ch = q % 2
+            if i == 1 and q == 2:
+                gain_send()
             t = term(i, q, z)[...].astype(F32)
             for way in range(2):
                 n = length(way, q)
@@ -448,6 +450,8 @@
             if q < 2:
                 sy[i, ch] = t.astype(BF16)
                 y_copy(i, ch).start()
+                if i == 1:
+                    gain_term(q, t, 0)
             else:
                 own_t[i, :, ch * FH : (ch + 1) * FH] = t
 
@@ -491,8 +495,7 @@
         cb = b * (1.0 / (1.0 - second_beta**adam_steps))
         w_out[rows, :] = w - learn_rate * (ca / (jnp.sqrt(cb) + 1e-08) + decay_rate * w)
 
-    scale_cot(0, inv(sums(0, 0)))
-    gradient(0, ((0, None),))
+    gradient(0, ((0, None),), (inv(sums(0, 0)),))
 
     for jy in range(MY):
         yl = flipped(ml, y_bits, jy)
@@ -508,7 +511,7 @@
                 zbuf[n, rows, :] = fold(p)
             return c
 
-        lax.fori_loop(0, MX, stats1, 0, unroll=2)
+        lax.fori_loop(0, MX, stats1, 0, unroll=4)
     ssend[1] = row_sums(4)
     def s2_copy(gg, j):
         return remote(ssend.at[1], srecv2.at[g * MP + m], s_s.at[1], s_r.at[1], at(gg=gg, mm=peer(j)))
@@ -527,10 +530,6 @@
     relayout_all(3, lambda i, gg: topb[gg, i], g)
     if H >= 2:
         ring_steps(0, 2)
-    if NY == 2:
-        w_copy().wait_recv()
-        for way in range(2):
-            wz_copy(way, 0).start()
     remote(topb.at[g], topb.at[1 - g], top_s, top_r, at(gg=1 - g)).wait_recv()
     relayout_all(3, lambda i, gg: topb[gg, i], 1 - g)
 
@@ -562,14 +561,12 @@
         + 2.0 * (rl * rv * sums(0, 5) + rl * rt * sums(1, 2) + rv * rt * sums(1, 3))
     )
     rj = inv(jnp.maximum(joined, 0.0))
-    scale_cot(1, rl * rj)
-    scale_cot(2, rv * rj)
-    scale_cot(3, rt * rj)
     for way in range(2):
-        for yo in range(2 - NY, 2):
-            wz_copy(way, yo).wait_recv()
-    gradient(1, ((1, 0), (2, 1), (3, 2)))
-
+        wz_copy(way).wait_recv()
+    gradient(1, ((1, 0), (2, 1), (3, 2)), (rl * rj, rv * rj, rt * rj))
+
+    if NY == 2:
+        w_copy().start()
     if H >= 4:
         ring_steps(0, 4)
     if H >= 2:
@@ -577,15 +574,16 @@
     ring_end(0)
     if H >= 3:
         ring_steps(1, 3)
-    for q in CHUNKS:
-        gain_term(q, term(1, q, z)[...].astype(F32), 0)
+    for q in range(2, 4):
+        gain_term(q, term(1, q, z)[...].astype(F32), 1)
     if H >= 4:
         ring_steps(1, 4)
     loads["m1"].wait()
     loads["m2"].wait()
     grad_end(0)
-    gain_send()
     adam(0)
+    if NY == 2:
+        w_copy().wait_recv()
     ring_end(1)
     grad_end(1)
     adam(1)
@@ -600,8 +598,7 @@
     if NY == 2:
         w_copy().wait_send()
     for way in range(2):
-        for yo in range(2 - NY, 2):
-            wz_copy(way, yo).wait_send()
+        wz_copy(way).wait_send()
 
     g_all().wait_recv()
     gsib_s[...] = jnp.sum(grecv[...].astype(F32), axis=0)
@@ -702,7 +699,7 @@
             pltpu.VMEM((2, 2, SH, FH), BF16),
             pltpu.VMEM((2, SH, F), F32),
             pltpu.VMEM((SH, F), F32),
-            pltpu.VMEM((3, 2, SH, F), BF16),
+            pltpu.VMEM((4, SH, F), BF16),
             pltpu.VMEM((2 * LT, HD), BF16),
             pltpu.VMEM((DP, 2 * LT, HD), BF16),
             pltpu.VMEM((2 * LT, HD), F32),
@@ -717,7 +714,7 @@
             dma((2, 2)), dma((2, 2, NQ, H)),
             dma((2,)), dma((2, 2)),
             dma, dma,
-            dma, dma((2, 2)),
+            dma, dma((2,)),
             dma, dma,
             dma, dma,
         ],

time: 70.3 us -> 69.4 us (0.987)
  Pallas kernels: 69.5 us -> 68.6 us
    pallas_call x1, Pallas kernels: 68.6 us -> 67.7 us  [shards(): pl.pallas_call(functools.partial(kernel, (NZ, NY, MP, MX, KVH, F, D, HC,...]
where the time goes in v6:
time: 69.4 us; the launch traced here: 69.2 us
  Pallas kernels  68.6 us (99%)
    pallas_call x1, Pallas kernels, shards(): pl.pallas_call(functools.partial(kernel, (NZ, NY, MP, MX, KVH, F, D, HC,...  67.7 us

profile of v6, /device:TPU:1, one launch (start us, length us, event | category | flops | bytes accessed | tf_op | source)
XLA Modules:
  0.0 69.2 jit_solution(8005787785103024089)
XLA Ops:
  0.6 67.7 %draft_step.1 = (f32[512,128]{1,0:T(8,128)S(1)}, f32[512,128]{1,0:T(8,128)S(1)}, f32[512,128]{1,0:T(8,128)S(1)}, f32[16,128]{1,0:T(8,128)S(1)}) custom-call(bf16[16,2,64,128]{3,2,1,0:T(8,128)(2,1)} %bitcast.71, bf16[4,64,1024]{2,1,0:T(8,128)(2,1)} %ck_hbm.1, bf16[4,64,1024]{2,1,0:T(8,128)(2,1)} %cv_hbm.1, bf16[128,128]{1,0:T(8,128)(2,1)} %bitcast.78, ...), custom_call_target="tpu_custom_call" | custom-call | flops 1073741824 | bytes 6291456 | tf_op jit(solution)/shard_map/draft_step/pallas_call | solution.py:656
  68.3 0.9 %hand_on.1 = (f32[512,128]{1,0:T(8,128)}, f32[512,128]{1,0:T(8,128)}, f32[512,128]{1,0:T(8,128)}, f32[16,128]{1,0:T(8,128)}) custom-call(f32[512,128]{1,0:T(8,128)S(1)} %get-tuple-element.12.refs_0_, f32[512,128]{1,0:T(8,128)S(1)} %get-tuple-element.13.refs_1_, f32[512,128]{1,0:T(8,128)S(1)} %get-tuple-element.14.refs_2_, ...), custom_call_target="tpu_custom_call" | custom-call | tf_op jit(solution)/shard_map/hand_on/pallas_call | solution.py:734

commit v7 on v6

--- a/solution.py
+++ b/solution.py
@@ -48,7 +48,7 @@
     jg_hbm, ng_hbm, ngn_hbm, w_hbm, m1_hbm, m2_hbm,
     w_out, m1_out, m2_out, gain_out,
     sk_ref, sv_ref, cot_ref, acc_ref, jg_ref, ng_ref, ngn_ref, rxq, kbuf, vbuf, outb, emb, lob, mib, topb, csend, cbuf, wbuf, m1buf, m2buf,
-    gpat, zbuf, ssend, srecv, srecv2, red, vx, ax, tb, sring, rring, sy, ry, own_t,
+    gpat, zbuf, ssend, srecv, srecv2, red, vx, vj, ax, aj, tb, sring, rring, sy, ry, own_t,
     w_two, wz, gsend, grecv, gsib_s, gsib_r,
     lsem, q_s, q_r, c_s, c_r, c2_s, c2_r, o_s, o_r, s_s, s_r, red_s, red_r, top_s, top_r,
     ring_s, ring_r, y_s, y_r, wx_s, wx_r, wz_s, wz_r, g_s, g_r, gx_s, gx_r,
@@ -183,20 +183,25 @@
 
     ssend[0] = row_sums(6)
 
-    def relayout(x):
+    def relayout(x, n):
         x = native_block(x)
+        if n > 0:
+            x = x * gpat[n - 1]
         a, b = x[0], x[1]
         return jnp.where(sub8, a, swap_halves(b)), jnp.where(sub8, swap_halves(a), b)
 
     def relayout_all(n, load, gg):
         def two(i, c):
-            parts = [relayout(load(2 * i + h, gg)) for h in range(2)]
+            parts = [relayout(load(2 * i + h, gg), n) for h in range(2)]
             rows = pl.ds(pl.multiple_of(gg * TH + i * 2 * SUB, 2 * SUB), 2 * SUB)
             for lp in range(LT // 2):
                 for k in range(2):
                     tile = jnp.concatenate([parts[0][k][lp], parts[1][k][lp]], axis=0)
                     lt = 2 * lp + k
-                    vx[n, rows, lt * HD : (lt + 1) * HD] = tile.astype(BF16)
+                    if n == 0:
+                        vx[rows, lt * HD : (lt + 1) * HD] = tile.astype(BF16)
+                    else:
+                        vj[n - 1, rows, lt * HD : (lt + 1) * HD] = tile.astype(BF16)
             return c
 
         lax.fori_loop(0, MP // 2, two, 0)
@@ -348,21 +353,22 @@
         here = pl.ds(pl.multiple_of(yy * SH, SH), SH)
         for b in range(YH):
             for x in range(MX):
-                ax[n, yy, b * MX + x] = (cbuf[x, b, here, :].astype(F32) * row).astype(BF16)
+                scaled = (cbuf[x, b, here, :].astype(F32) * row).astype(BF16)
+                if n == 0:
+                    ax[yy, b * MX + x] = scaled
+                else:
+                    aj[yy, b * MX + x, :, (n - 1) * T : n * T] = scaled
 
     scale = (2.0 * D) ** -0.5
 
-    def tile(i, yy, ch, terms):
+    def tile(i, yy, ch):
         for h in range(2):
             cols = slice(ch * FH + h * FH // 2, ch * FH + (h + 1) * FH // 2)
-            total = None
-            for n_x, gain in terms:
-                part = jnp.dot(
-                    ax[n_x, yy].reshape(NZ * SH, T), vx[n_x, :, cols], preferred_element_type=F32
-                )
-                if gain is not None:
-                    part = part * jg_ref[gain : gain + 1, cols]
-                total = part if total is None else total + part
+            if i == 0:
+                total = jnp.dot(ax[yy].reshape(NZ * SH, T), vx[:, cols], preferred_element_type=F32)
+            else:
+                gained = vj[:, :, cols].reshape(3 * T, FH // 2)
+                total = jnp.dot(aj[yy].reshape(NZ * SH, 3 * T), gained, preferred_element_type=F32)
             total = (total * (ng_ref[i : i + 1, cols] * scale)).astype(BF16)
             tb[i, yy, ch, :, :, h * FH // 2 : (h + 1) * FH // 2] = total.reshape(NZ, SH, FH // 2)
 
@@ -425,9 +431,9 @@
     def gradient(i, terms, rows):
         for q in CHUNKS:
             if q % 2 == 0:
-                for (n, _), row in zip(terms, rows):
+                for n, row in zip(terms, rows):
                     scale_cot(n, row, y_of(q))
-            tile(i, y_of(q), q % 2, terms)
+            tile(i, y_of(q), q % 2)
             ring_step(i, 1, q)
 
     def y_copy(i, ch):
@@ -495,7 +501,7 @@
         cb = b * (1.0 / (1.0 - second_beta**adam_steps))
         w_out[rows, :] = w - learn_rate * (ca / (jnp.sqrt(cb) + 1e-08) + decay_rate * w)
 
-    gradient(0, ((0, None),), (inv(sums(0, 0)),))
+    gradient(0, (0,), (inv(sums(0, 0)),))
 
     for jy in range(MY):
         yl = flipped(ml, y_bits, jy)
@@ -546,7 +552,7 @@
 
     @pl.when(sends_cot)
     def _():
-        some = ax.at[0, 0, 0 : (MY - 1) * CW // SH]
+        some = ax.at[0, 0 : (MY - 1) * CW // SH]
         remote(some, some, c_s, c_r.at[0], at(mm=peer(1))).wait_send()
 
     s2_all().wait_recv()
@@ -563,7 +569,7 @@
     rj = inv(jnp.maximum(joined, 0.0))
     for way in range(2):
         wz_copy(way).wait_recv()
-    gradient(1, ((1, 0), (2, 1), (3, 2)), (rl * rj, rv * rj, rt * rj))
+    gradient(1, (1, 2, 3), (rl * rj, rv * rj, rt * rj))
 
     if NY == 2:
         w_copy().start()
@@ -690,8 +696,10 @@
             pltpu.VMEM((MP, SUB, TH), F32),
             pltpu.VMEM((2 * MP, SUB, TH), F32),
             pltpu.VMEM((2, 2, SUB, TH), F32),
-            pltpu.VMEM((4, T, F), BF16),
-            pltpu.VMEM((4, NY, NZ, SH, T), BF16),
+            pltpu.VMEM((T, F), BF16),
+            pltpu.VMEM((3, T, F), BF16),
+            pltpu.VMEM((NY, NZ, SH, T), BF16),
+            pltpu.VMEM((NY, NZ, SH, 3 * T), BF16),
             pltpu.VMEM((2, NY, 2, NZ, SH, FH), BF16),
             pltpu.VMEM((2, 2, NQ, max(H - 1, 1), SH, FH), BF16),
             pltpu.VMEM((2, 2, NQ, H, SH, FH), BF16),

time: 69.4 us -> 68.8 us (level)
  no operation moved by 1% of the time
where the time goes in v7:
time: 68.8 us; the launch traced here: 68.6 us
  Pallas kernels  68 us (99%)
    pallas_call x1, Pallas kernels, shards(): pl.pallas_call(functools.partial(kernel, (NZ, NY, MP, MX, KVH, F, D, HC,...  67.1 us

profile of v7, /device:TPU:1, one launch (start us, length us, event | category | flops | bytes accessed | tf_op | source)
XLA Modules:
  0.0 68.6 jit_solution(64954867690686446)
XLA Ops:
  0.6 67.1 %draft_step.1 = (f32[512,128]{1,0:T(8,128)S(1)}, f32[512,128]{1,0:T(8,128)S(1)}, f32[512,128]{1,0:T(8,128)S(1)}, f32[16,128]{1,0:T(8,128)S(1)}) custom-call(bf16[16,2,64,128]{3,2,1,0:T(8,128)(2,1)} %bitcast.71, bf16[4,64,1024]{2,1,0:T(8,128)(2,1)} %ck_hbm.1, bf16[4,64,1024]{2,1,0:T(8,128)(2,1)} %cv_hbm.1, bf16[128,128]{1,0:T(8,128)(2,1)} %bitcast.78, ...), custom_call_target="tpu_custom_call" | custom-call | flops 1073741824 | bytes 6291456 | tf_op jit(solution)/shard_map/draft_step/pallas_call | solution.py:662
  67.7 0.9 %hand_on.1 = (f32[512,128]{1,0:T(8,128)}, f32[512,128]{1,0:T(8,128)}, f32[512,128]{1,0:T(8,128)}, f32[16,128]{1,0:T(8,128)}) custom-call(f32[512,128]{1,0:T(8,128)S(1)} %get-tuple-element.12.refs_0_, f32[512,128]{1,0:T(8,128)S(1)} %get-tuple-element.13.refs_1_, f32[512,128]{1,0:T(8,128)S(1)} %get-tuple-element.14.refs_2_, ...), custom_call_target="tpu_custom_call" | custom-call | tf_op jit(solution)/shard_map/hand_on/pallas_call | solution.py:742
